TPU v7x, 32 devices: a whole 2x2x4 slice. The times are simulated.
32 devices in a mesh: groups: 2 (over x), res: 16 (over z, y, core).
Axes of the slice: x: 2, y: 2, z: 4, core: 2. Of those that a mesh axis runs over, the one named last changes fastest.
Arguments:
- pair_left: bfloat16 [2048, 64, 128], P(('groups', 'res')), parts along dimension 0, may hold values from -6 to 6
- pair_right: bfloat16 [2048, 256, 128], P(('groups', 'res')), parts along dimension 0, may hold values from -6 to 6
- pair_block: bfloat16 [512, 64, 128], P(('groups', 'res')), parts along dimension 0, may hold values from -6 to 6
- grad_out: bfloat16 [512, 64, 128], P(('groups', 'res')), parts along dimension 0, may hold values from -6 to 6
- norm_gain: float32 [128], replicated, may hold values from 0.25 to 1.75
- norm_bias: float32 [128], replicated, may hold values from -3 to 3
- weight_left: bfloat16 [128, 128], replicated, may hold values from -0.5 to 0.5
- gate_left: bfloat16 [128, 128], replicated, may hold values from -0.5 to 0.5
- weight_right: bfloat16 [128, 128], replicated, may hold values from -0.5 to 0.5
- gate_right: bfloat16 [128, 128], replicated, may hold values from -0.5 to 0.5
- tri_gain: float32 [128], replicated, may hold values from 0.25 to 1.75
- tri_bias: float32 [128], replicated, may hold values from -3 to 3
- weight_out: bfloat16 [128, 128], replicated, may hold values from -0.5 to 0.5
- gate_out: bfloat16 [128, 128], replicated, may hold values from -0.5 to 0.5
- tile_left: int32 [32, 4], P(('groups', 'res')), parts along dimension 0, may hold values 0 or 1
- tile_right: int32 [32, 16], P(('groups', 'res')), parts along dimension 0, may hold values 0 or 1
- chain_rows: int32 [2048], P(('groups', 'res')), parts along dimension 0, may hold values from 0 to 5, never falling along the last dimension, each value on 1 to 256 neighbouring positions
- chain_slab: int32 [128], P('groups'), parts along dimension 0, may hold values from 0 to 5, never falling along the last dimension, each value on 1 to 16 neighbouring positions
- chain_cols: int32 [512], P('groups'), parts along dimension 0, may hold values from 0 to 5, never falling along the last dimension, each value on 1 to 64 neighbouring positions
Outputs:
- grad_left: bfloat16 [2048, 64, 128], P(('groups', 'res')), parts along dimension 0
- grad_right: bfloat16 [2048, 256, 128], P(('groups', 'res')), parts along dimension 0
- grad_block: bfloat16 [512, 64, 128], P(('groups', 'res')), parts along dimension 0
There are 2 independent parts, one for each index of `groups`. A program takes and returns all parts, laid end to end along the dimension named above; an argument that names none is the same for every part. Nothing has to cross between parts.
All inputs are finite; a program needn't handle non-finite values. No bound on the sum of `tile_left` or of `tile_right` on one device may be relied on, other than what follows from the above.
Results may differ from a plain program's by a relative error of at most 0.017.
Values may be sent and summed in bfloat16 or wider, within the bound.
A program may use at most 320 MiB of HBM per device.

v0:
```python
import jax
import jax.numpy as jnp
from jax import lax
from jax.sharding import PartitionSpec as P


def layer_norm(values, gain, bias):
    values = values.astype(jnp.float32)
    center = jnp.mean(values, axis=-1, keepdims=True)
    spread = jnp.mean(jnp.square(values - center), axis=-1, keepdims=True)
    return (values - center) * lax.rsqrt(spread + 1e-05) * gain + bias


def projection(pair, mask, norm_gain, norm_bias, weight, gate):
    normed = layer_norm(pair, norm_gain, norm_bias).astype(jnp.bfloat16)
    value = jnp.dot(normed, weight, preferred_element_type=jnp.float32)
    gating = jax.nn.sigmoid(jnp.dot(normed, gate, preferred_element_type=jnp.float32))
    return mask[..., None] * gating * value


def output_gate(tri, pair, norm_gain, norm_bias, tri_gain, tri_bias, weight_out, gate_out):
    normed = layer_norm(pair, norm_gain, norm_bias).astype(jnp.bfloat16)
    gating = jax.nn.sigmoid(jnp.dot(normed, gate_out, preferred_element_type=jnp.float32))
    scaled = layer_norm(tri, tri_gain, tri_bias).astype(jnp.bfloat16)
    return gating * jnp.dot(scaled, weight_out, preferred_element_type=jnp.float32)


def local(
    pair_left,
    pair_right,
    pair_block,
    grad_out,
    norm_gain,
    norm_bias,
    weight_left,
    gate_left,
    weight_right,
    gate_right,
    tri_gain,
    tri_bias,
    weight_out,
    gate_out,
    tile_left,
    tile_right,
    chain_rows,
    chain_slab,
    chain_cols,
):
    slab_rows = pair_left.shape[1]
    block_cols = pair_block.shape[0]
    tile_rows = slab_rows // tile_left.shape[1]
    same_left = (chain_rows[:, None] == chain_slab[None, :]).astype(jnp.int32)
    mask_left = jnp.maximum(jnp.repeat(tile_left, tile_rows, axis=1), same_left).astype(jnp.float32)
    same_right = (chain_rows[:, None] == chain_cols[None, :]).astype(jnp.int32)
    mask_right = jnp.maximum(jnp.repeat(tile_right, block_cols, axis=1), same_right).astype(
        jnp.float32
    )
    left_full, left_back = jax.vjp(
        lambda pair: projection(pair, mask_left, norm_gain, norm_bias, weight_left, gate_left),
        pair_left,
    )
    right_full, right_back = jax.vjp(
        lambda pair: projection(pair, mask_right, norm_gain, norm_bias, weight_right, gate_right),
        pair_right,
    )
    left = left_full.astype(jnp.bfloat16)
    right = right_full.astype(jnp.bfloat16)
    tri = lax.psum_scatter(
        jnp.einsum("kic,kjc->jic", left, right, preferred_element_type=jnp.float32).astype(jnp.bfloat16),
        "res",
        scatter_dimension=0,
        tiled=True,
    ).astype(jnp.float32)
    result, out_back = jax.vjp(
        lambda product, pair: output_gate(
            product, pair, norm_gain, norm_bias, tri_gain, tri_bias, weight_out, gate_out
        ),
        tri,
        pair_block,
    )
    grad_tri, block_grad = out_back(grad_out.astype(jnp.float32))
    sent = grad_tri.astype(jnp.bfloat16)

    gathered = lax.all_gather(sent, "res", axis=0, tiled=True)
    total_left = jnp.einsum("jic,kjc->kic", gathered, right, preferred_element_type=jnp.float32)
    total_right = jnp.einsum("kic,jic->kjc", left, gathered, preferred_element_type=jnp.float32)
    (grad_left,) = left_back(total_left)
    (grad_right,) = right_back(total_right)
    return (grad_left, grad_right, block_grad)


def solution(mesh):
    placed = (
        P(("groups", "res"), None, None),
        P(("groups", "res"), None, None),
        P(("groups", "res"), None, None),
        P(("groups", "res"), None, None),
        P(),
        P(),
        P(),
        P(),
        P(),
        P(),
        P(),
        P(),
        P(),
        P(),
        P(("groups", "res"), None),
        P(("groups", "res"), None),
        P(("groups", "res")),
        P("groups"),
        P("groups"),
    )
    return jax.shard_map(
        local,
        mesh=mesh,
        in_specs=placed,
        out_specs=(
            P(("groups", "res"), None, None),
            P(("groups", "res"), None, None),
            P(("groups", "res"), None, None),
        ),
        check_vma=False,
    )
```

profile of v0, /device:TPU:11, one launch (start us, length us, event | category | flops | bytes accessed | tf_op | source)
XLA Modules:
  0.0 296.8 jit_solution(1043107018147930374)
XLA Ops:
  7.2 1.8 convert_reduce_fusion.1
  9.1 2.3 fusion.33
  11.5 0.7 broadcast_in_dim.12
  12.2 0.1 max.28
  12.3 6.4 %copy.35 = bf16[64,256,128]{1,2,0:T(8,128)(2,1)} copy(bf16[64,256,128]{2,1,0:T(8,128)(2,1)} %param.20) | data formatting | bytes 8388608 | tf_op args[1]
  18.7 3.4 %convert_reduce_fusion = f32[64,256]{1,0:T(8,128)S(1)} fusion(bf16[64,256,128]{1,2,0:T(8,128)(2,1)} %copy.35), kind=kLoop, calls=%fused_computation.2 | loop fusion | flops 4177920 | bytes 4259840 | tf_op jit(solution)/shard_map/jvp()/reduce_sum | solution.py:9
  22.1 1.6 fusion.8
  24.0 4.9 %add_divide_fusion = f32[64,256,128]{2,1,0:T(8,128)S(1)} fusion(bf16[128,128]{1,0:T(8,128)(2,1)S(1)} %copy-done.18, bf16[64,256,128]{1,2,0:T(8,128)(2,1)} %copy.35, f32[128]{0:T(128)S(1)} %copy-done.20, f32[128]{0:T(128)S(1)} %copy-done.19, f32[64,256]{1,0:T(8,128)S(1)} %fusion.111, f32[64,256]{1,0:T(8,128)S(1)} %broadcast_multiply_fusion), kind=kOutput, calls=%fused_computation.26 | convolution fusion | flops 555745280 | bytes 12747776 | tf_op jit(solution)/shard_map/jvp()/dot_general | solution.py:17
  28.9 7.3 %multiply_convert_fusion = (bf16[64,256,128]{2,1,0:T(8,128)(2,1)}, f32[64,256,128]{2,1,0:T(8,128)}) fusion(f32[64,256,128]{2,1,0:T(8,128)S(1)} %add_divide_fusion, f32[64,256]{1,0:T(8,128)S(1)} %maximum_convert_fusion, bf16[128,128]{1,0:T(8,128)(2,1)S(1)} %copy-done, bf16[64,256,128]{1,2,0:T(8,128)(2,1)S(1)} %copy-done.2, f32[128]{0:T(128)S(1)} %copy-done.20, ...), kind=kOutput, calls=%fused_computation.25 | convolution fusion | flops 555745280 | bytes 25396224 | tf_op jit(solution)/shard_map/jvp()/dot_general | solution.py:16
  36.2 6.9 %copy.41 = bf16[64,256,128]{1,0,2:T(8,128)(2,1)} copy(bf16[64,256,128]{2,1,0:T(8,128)(2,1)} %get-tuple-element.17) | data formatting | bytes 8388608 | tf_op jit(solution)/shard_map/convert_element_type | solution.py:67
  43.1 1.3 add_divide_fusion.1
  44.5 1.2 copy-done.9
  45.8 3.2 %multiply_convert_fusion.1 = (bf16[64,64,128]{2,1,0:T(8,128)(2,1)S(1)}, f32[64,64,128]{2,1,0:T(8,128)}) fusion(f32[64,64,128]{2,1,0:T(8,128)S(1)} %add_divide_fusion.1, f32[64,64]{1,0:T(8,128)S(1)} %maximum_convert_fusion.1, bf16[128,128]{1,0:T(8,128)(2,1)S(1)} %copy-done.15, bf16[64,64,128]{2,1,0:T(8,128)(2,1)S(1)} %copy-done.7, f32[128]{0:T(128)S(1)} %copy-done.20, ...), kind=kOutput, calls=%fused_computation.58 | convolution fusion | flops 138936320 | bytes 6374400 | tf_op jit(solution)/shard_map/jvp()/dot_general | solution.py:16
  48.9 3.8 %copy.45 = bf16[64,64,128]{1,0,2:T(8,128)(2,1)} copy(bf16[64,64,128]{2,1,0:T(8,128)(2,1)S(1)} %get-tuple-element.19) | data formatting | bytes 2097152 | tf_op jit(solution)/shard_map/convert_element_type | solution.py:66
  52.7 6.1 %fusion.140 = bf16[128,256,64]{1,2,0:T(8,128)(2,1)} fusion(bf16[64,64,128]{1,0,2:T(8,128)(2,1)} %copy.45, bf16[64,256,128]{1,0,2:T(8,128)(2,1)} %copy.41), kind=kOutput, calls=%fused_computation.165 | convolution fusion | flops 268435456 | bytes 9437184 | tf_op jit(solution)/shard_map/kic,kjc->jic/dot_general | solution.py:69
  58.8 7.4 %copy.40 = bf16[128,256,64]{0,2,1:T(8,128)(2,1)} copy(bf16[128,256,64]{1,2,0:T(8,128)(2,1)} %fusion.140) | data formatting | bytes 8388608 | tf_op jit(solution)/shard_map/kic,kjc->jic/dot_general | solution.py:69
  66.2 0.2 all-gather.2.cloned.1.call-start
  66.5 0.7 copy-done.12
  67.1 0.2 convert_reduce_fusion.3
  67.3 0.4 fusion.82
  67.8 0.5 fusion.54
  68.2 69.7 %reduce-scatter.2.cloned.1.call-done = bf16[16,64,128]{2,1,0:T(8,128)(2,1)} async-done(((bf16[256,64,128]{2,1,0:T(8,128)(2,1)}), bf16[16,64,128]{2,1,0:T(8,128)(2,1)}) %reduce-scatter.2.cloned.1.call-update) | async-done | bytes 262160 | tf_op jit(solution)/shard_map/reduce_scatter | solution.py:68
  137.9 1.2 convert_reduce_fusion.2
  139.1 1.3 fusion.87
  140.5 1.6 multiply_reduce_fusion.1
  142.1 1.5 fusion.76
  143.6 2.3 fusion.79
  145.9 1.9 multiply_reduce_fusion
  147.7 0.5 fusion.74
  148.3 1.3 fusion.81
  149.6 48.5 %all-gather.2.cloned.1.call-done = bf16[256,64,128]{2,1,0:T(8,128)(2,1)} async-done(((bf16[16,64,128]{2,1,0:T(8,128)(2,1)}), bf16[256,64,128]{2,1,0:T(8,128)(2,1)}) %all-gather.2.cloned.1.call-update) | async-done | bytes 4194320 | tf_op jit(solution)/shard_map/all_gather | solution.py:84
  198.1 12.9 %copy.42 = bf16[256,64,128]{1,0,2:T(8,128)(2,1)} copy(bf16[256,64,128]{2,1,0:T(8,128)(2,1)} %all-gather.2.cloned.1.call-done) | data formatting | bytes 8388608 | tf_op jit(solution)/shard_map/all_gather | solution.py:84
  211.0 8.3 %fusion.138 = f32[128,64,64]{2,1,0:T(8,128)} fusion(bf16[64,256,128]{1,0,2:T(8,128)(2,1)} %copy.41, bf16[256,64,128]{1,0,2:T(8,128)(2,1)} %copy.42), kind=kOutput, calls=%fused_computation.163 | convolution fusion | flops 268435456 | bytes 10485760 | tf_op jit(solution)/shard_map/jic,kjc->kic/dot_general | solution.py:85
  219.3 7.9 %fusion.139 = f32[128,256,64]{1,2,0:T(8,128)} fusion(bf16[256,64,128]{1,0,2:T(8,128)(2,1)S(1)} %copy-done.4, bf16[64,64,128]{1,0,2:T(8,128)(2,1)} %copy.45), kind=kOutput, calls=%fused_computation.164 | convolution fusion | flops 268435456 | bytes 13631488 | tf_op jit(solution)/shard_map/kic,jic->kjc/dot_general | solution.py:86
  227.2 4.8 %copy.43 = f32[128,64,64]{0,2,1:T(8,128)} copy(f32[128,64,64]{2,1,0:T(8,128)} %fusion.138) | data formatting | bytes 4194304 | tf_op jit(solution)/shard_map/jic,kjc->kic/dot_general | solution.py:85
  231.9 3.7 %fusion.47 = bf16[64,64,128]{2,1,0:T(8,128)(2,1)S(1)} fusion(f32[64,64,128]{2,1,0:T(8,128)} %copy-done.9, f32[64,64,128]{2,1,0:T(8,128)} %get-tuple-element.20, f32[128,64,64]{0,2,1:T(8,128)} %copy.43, f32[64,64]{1,0:T(8,128)S(1)} %maximum_convert_fusion.1, bf16[128,128]{1,0:T(8,128)(2,1)S(1)} %copy-done.16), kind=kOutput, calls=%fused_computation.61 | convolution fusion | flops 137363456 | bytes 7389184 | tf_op jit(solution)/shard_map/transpose(jvp())/dot_general | solution.py:17
  235.7 0.3 copy-done.10
  236.0 3.7 %fusion.45 = (f32[64,64]{1,0:T(8,128)S(1)}, f32[64,64]{1,0:T(8,128)S(1)}, bf16[64,64,128]{2,1,0:T(8,128)(2,1)}) fusion(f32[128]{0:T(128)S(1)} %copy-done.19, f32[64,64]{1,0:T(8,128)S(1)} %fusion.126, f32[64,64]{1,0:T(8,128)S(1)} %broadcast_multiply_fusion.1, bf16[64,64,128]{2,1,0:T(8,128)(2,1)S(1)} %copy-done.7, bf16[64,64,128]{2,1,0:T(8,128)(2,1)S(1)} %fusion.47, ...), kind=kOutput, calls=%fused_computation.57 | convolution fusion | flops 140500992 | bytes 7455232 | tf_op jit(solution)/shard_map/transpose(jvp())/dot_general | solution.py:16
  239.8 1.8 fusion.29
  241.6 9.3 %copy.46 = f32[128,256,64]{0,1,2:T(8,128)} copy(f32[128,256,64]{1,2,0:T(8,128)} %fusion.139) | data formatting | bytes 16777216 | tf_op jit(solution)/shard_map/kic,jic->kjc/dot_general | solution.py:86
  250.9 11.8 %fusion.14 = bf16[64,256,128]{1,2,0:T(8,128)(2,1)} fusion(f32[64,256,128]{2,1,0:T(8,128)} %copy-done.5, f32[64,256,128]{2,1,0:T(8,128)} %get-tuple-element.18, f32[128,256,64]{0,1,2:T(8,128)} %copy.46, f32[64,256]{1,0:T(8,128)S(1)} %maximum_convert_fusion, bf16[128,128]{1,0:T(8,128)(2,1)S(1)} %copy-done.18), kind=kOutput, calls=%fused_computation.17 | convolution fusion | flops 547356672 | bytes 29458432 | tf_op jit(solution)/shard_map/transpose(jvp())/dot_general | solution.py:17
  262.7 1.6 copy-done.6
  264.3 9.3 %fusion.20 = (f32[64,256]{1,0:T(8,128)S(1)}, f32[64,256]{1,0:T(8,128)S(1)}, bf16[64,256,128]{1,2,0:T(8,128)(2,1)}) fusion(f32[128]{0:T(128)S(1)} %copy-done.19, f32[64,256]{1,0:T(8,128)S(1)} %fusion.111, f32[64,256]{1,0:T(8,128)S(1)} %broadcast_multiply_fusion, bf16[64,256,128]{1,2,0:T(8,128)(2,1)S(1)} %copy-done.3, bf16[64,256,128]{1,2,0:T(8,128)(2,1)} %fusion.14, ...), kind=kOutput, calls=%fused_computation.24 | convolution fusion | flops 562003968 | bytes 29721088 | tf_op jit(solution)/shard_map/transpose(jvp())/dot_general | solution.py:16
  273.6 2.0 fusion.4
  275.7 0.1 copy-done.11
  275.8 4.4 %fusion.7 = bf16[64,256,128]{1,2,0:T(8,128)(2,1)} fusion(bf16[64,256,128]{1,2,0:T(8,128)(2,1)S(1)} %copy-done.3, bf16[64,256,128]{1,2,0:T(8,128)(2,1)S(1)} %copy-done.11, f32[64,256]{1,0:T(8,128)S(1)} %add_multiply_fusion, f32[64,256]{1,0:T(8,128)S(1)} %multiply_multiply_fusion, f32[128]{0:T(128)S(1)} %copy-done.19, f32[64,256]{1,0:T(8,128)S(1)} %fusion.111, ...), kind=kLoop, calls=%fused_computation.10 | loop fusion | flops 18874368 | bytes 12845568 | tf_op jit(solution)/shard_map/transpose(jvp())/convert_element_type | solution.py:8
  280.2 6.4 %copy.47 = bf16[64,256,128]{2,1,0:T(8,128)(2,1)} copy(bf16[64,256,128]{1,2,0:T(8,128)(2,1)} %fusion.7) | data formatting | bytes 8388608
  286.7 3.3 %fusion.32 = bf16[64,64,128]{2,1,0:T(8,128)(2,1)} fusion(bf16[64,64,128]{2,1,0:T(8,128)(2,1)S(1)} %copy-done.7, bf16[64,64,128]{2,1,0:T(8,128)(2,1)S(1)} %copy-done.13, f32[64,64]{1,0:T(8,128)S(1)} %add_multiply_fusion.1, f32[64,64]{1,0:T(8,128)S(1)} %multiply_multiply_fusion.1, f32[128]{0:T(128)S(1)} %copy-done.19, f32[64,64]{1,0:T(8,128)S(1)} %fusion.126, ...), kind=kLoop, calls=%fused_computation.43 | loop fusion | flops 4718592 | bytes 3211776 | tf_op jit(solution)/shard_map/transpose(jvp())/convert_element_type | solution.py:8
  (74 shorter events, 0.7 us)
Async XLA Ops:
  7.2 21.7 %copy-start = (bf16[128,128]{1,0:T(8,128)(2,1)S(1)}, bf16[128,128]{1,0:T(8,128)(2,1)}, u32[]{:S(2)}) copy-start(bf16[128,128]{1,0:T(8,128)(2,1)} %param.27) | copy-start | bytes 98308
  7.2 130.7 %reduce-scatter.2.cloned.1.call-start = ((), (), s32[]{:S(2)}) async-start(), calls=%async_computation.1 | async-start | bytes 4456448 | tf_op jit(solution)/shard_map/reduce_scatter | solution.py:68
  18.6 3.4 %copy-start.1 = (bf16[64,256,128]{1,2,0:T(8,128)(2,1)S(1)}, bf16[64,256,128]{1,2,0:T(8,128)(2,1)}, u32[]{:S(2)}) copy-start(bf16[64,256,128]{1,2,0:T(8,128)(2,1)} %copy.35) | copy-start | bytes 12582916
  18.6 5.0 %copy-start.25 = (s32[1,16]{1,0:T(1,128)S(1)}, s32[1,16]{1,0:T(1,128)}, u32[]{:S(2)}) copy-start(s32[1,16]{1,0:T(1,128)} %param.34) | copy-start | bytes 196
  18.6 5.2 %copy-start.21 = (s32[64]{0:T(128)S(1)}, s32[64]{0:T(128)}, u32[]{:S(2)}) copy-start(s32[64]{0:T(128)} %param.35) | copy-start | bytes 772
  18.6 5.2 %copy-start.22 = (s32[256]{0:T(256)S(1)}, s32[256]{0:T(256)}, u32[]{:S(2)}) copy-start(s32[256]{0:T(256)} %param.37) | copy-start | bytes 3076
  18.6 5.3 %copy-start.18 = (bf16[128,128]{1,0:T(8,128)(2,1)S(1)}, bf16[128,128]{1,0:T(8,128)(2,1)}, u32[]{:S(2)}) copy-start(bf16[128,128]{1,0:T(8,128)(2,1)} %param.28) | copy-start | bytes 98308
  18.6 5.3 %copy-start.19 = (f32[128]{0:T(128)S(1)}, f32[128]{0:T(128)}, u32[]{:S(2)}) copy-start(f32[128]{0:T(128)} %param.23) | copy-start | bytes 1540
  18.7 5.3 %copy-start.20 = (f32[128]{0:T(128)S(1)}, f32[128]{0:T(128)}, u32[]{:S(2)}) copy-start(f32[128]{0:T(128)} %param.24) | copy-start | bytes 1540
  24.0 4.9 %copy-start.2 = (bf16[64,256,128]{1,2,0:T(8,128)(2,1)S(1)}, bf16[64,256,128]{1,2,0:T(8,128)(2,1)}, u32[]{:S(2)}) copy-start(bf16[64,256,128]{1,2,0:T(8,128)(2,1)} %copy.35) | copy-start | bytes 12582916
  28.9 7.3 %copy-start.5 = (f32[64,256,128]{2,1,0:T(8,128)}, f32[64,256,128]{2,1,0:T(8,128)S(1)}, u32[]{:S(2)}) copy-start(f32[64,256,128]{2,1,0:T(8,128)S(1)} %add_divide_fusion) | copy-start | bytes 25165828
  36.2 6.9 %copy-start.7 = (bf16[64,64,128]{2,1,0:T(8,128)(2,1)S(1)}, bf16[64,64,128]{2,1,0:T(8,128)(2,1)}, u32[]{:S(2)}) copy-start(bf16[64,64,128]{2,1,0:T(8,128)(2,1)} %param.19) | copy-start | bytes 3145732
  36.2 6.9 %copy-start.16 = (bf16[128,128]{1,0:T(8,128)(2,1)S(1)}, bf16[128,128]{1,0:T(8,128)(2,1)}, u32[]{:S(2)}) copy-start(bf16[128,128]{1,0:T(8,128)(2,1)} %param.26) | copy-start | bytes 98308
  43.1 1.3 copy-start.23
  43.1 2.6 copy-start.15
  44.4 1.3 copy-start.9
  66.2 0.9 copy-start.12
  66.2 1.6 copy-start.26
  66.2 74.3 %copy-start.14 = (bf16[16,64,128]{2,1,0:T(8,128)(2,1)S(1)}, bf16[16,64,128]{2,1,0:T(8,128)(2,1)}, u32[]{:S(2)}) copy-start(bf16[16,64,128]{2,1,0:T(8,128)(2,1)} %param.22) | copy-start | bytes 786436
  66.2 74.3 %copy-start.17 = (bf16[128,128]{1,0:T(8,128)(2,1)S(1)}, bf16[128,128]{1,0:T(8,128)(2,1)}, u32[]{:S(2)}) copy-start(bf16[128,128]{1,0:T(8,128)(2,1)} %param.31) | copy-start | bytes 98308
  66.2 74.3 %copy-start.24 = (f32[128]{0:T(128)S(1)}, f32[128]{0:T(128)}, u32[]{:S(2)}) copy-start(f32[128]{0:T(128)} %param.29) | copy-start | bytes 1540
  66.2 79.6 %copy-start.27 = (f32[128]{0:T(128)S(1)}, f32[128]{0:T(128)}, u32[]{:S(2)}) copy-start(f32[128]{0:T(128)} %param.30) | copy-start | bytes 1540
  66.2 131.8 %all-gather.2.cloned.1.call-start = ((), (), s32[]{:S(2)}) async-start(), calls=%async_computation.2 | async-start | bytes 4456448 | tf_op jit(solution)/shard_map/all_gather | solution.py:84
  211.0 8.3 %copy-start.4 = (bf16[256,64,128]{1,0,2:T(8,128)(2,1)S(1)}, bf16[256,64,128]{1,0,2:T(8,128)(2,1)}, u32[]{:S(2)}) copy-start(bf16[256,64,128]{1,0,2:T(8,128)(2,1)} %copy.42) | copy-start | bytes 12582916
  231.9 3.7 %copy-start.8 = (f32[128,64,64]{0,2,1:T(8,128)S(1)}, f32[128,64,64]{0,2,1:T(8,128)}, u32[]{:S(2)}) copy-start(f32[128,64,64]{0,2,1:T(8,128)} %copy.43) | copy-start | bytes 6291460
  231.9 4.1 %copy-start.10 = (f32[64,64,128]{2,1,0:T(8,128)S(1)}, f32[64,64,128]{2,1,0:T(8,128)}, u32[]{:S(2)}) copy-start(f32[64,64,128]{2,1,0:T(8,128)} %copy-done.9) | copy-start | bytes 6291460
  250.9 11.8 %copy-start.3 = (bf16[64,256,128]{1,2,0:T(8,128)(2,1)S(1)}, bf16[64,256,128]{1,2,0:T(8,128)(2,1)}, u32[]{:S(2)}) copy-start(bf16[64,256,128]{1,2,0:T(8,128)(2,1)} %copy.35) | copy-start | bytes 12582916
  250.9 13.4 %copy-start.6 = (f32[128,256,64]{0,1,2:T(8,128)S(1)}, f32[128,256,64]{0,1,2:T(8,128)}, u32[]{:S(2)}) copy-start(f32[128,256,64]{0,1,2:T(8,128)} %copy.46) | copy-start | bytes 25165828
  273.6 2.2 copy-start.11
  280.2 6.5 %copy-start.13 = (bf16[64,64,128]{2,1,0:T(8,128)(2,1)S(1)}, bf16[64,64,128]{2,1,0:T(8,128)(2,1)}, u32[]{:S(2)}) copy-start(bf16[64,64,128]{2,1,0:T(8,128)(2,1)} %get-tuple-element.22) | copy-start | bytes 3145732
Sparse Core Ops, SparseCore 0:
  66.3 71.5 reduce-scatter.1
  146.0 52.0 all-gather.1
where the time goes:
time: 299 us; the launch traced here: 297 us
  waiting for transfers between devices  118 us (39%)
  matrix products  71.4 us (24%)
  local copies, waits for them, and re-layouts  62.8 us (21%)
  other arithmetic  29.6 us (10%)
  between operations  14.5 us (5%)
    reduce_scatter x1, waiting for transfers between devices, local(): lax.psum_scatter(jnp.einsum('kic,kjc->jic', left, right, preferred_elemen...  69.7 us
    all_gather x1, waiting for transfers between devices, local(): gathered = lax.all_gather(sent, 'res', axis=0, tiled=True)  48.5 us
    dot_general x4, matrix products, projection(): value = jnp.dot(normed, weight, preferred_element_type=jnp.float32)  23.5 us
    dot_general x4, matrix products, projection(): jnp.dot(normed, gate, preferred_element_type=jnp.float32)  21.7 us
    unnamed x58, local copies, waits for them, and re-layouts  16.8 us
    all_gather x1, local copies, waits for them, and re-layouts, local(): gathered = lax.all_gather(sent, 'res', axis=0, tiled=True)  12.9 us
    reduce_sum x8, other arithmetic, layer_norm(): spread = jnp.mean(jnp.square(values - center), axis=-1, keepdims=True)  11.4 us
    dot_general x1, local copies, waits for them, and re-layouts, local(): jnp.einsum('kic,jic->kjc', left, gathered, preferred_element_type=jnp.flo...  9.25 us
  transfers between devices with their start and end apart: 2, of which 2 were waited for; matrix products, arithmetic and copies ran while one was open for 2% of the time, Pallas kernels for 0%

commit v1 on v0

--- a/solution.py
+++ b/solution.py
@@ -1,7 +1,163 @@
+import functools
+
 import jax
 import jax.numpy as jnp
 from jax import lax
+from jax.experimental import pallas as pl
+from jax.experimental.pallas import tpu as pltpu
 from jax.sharding import PartitionSpec as P
+
+
+MESH = pl.DeviceIdType.MESH
+VMEM_LIMIT = 48 * 1024 * 1024
+
+
+def bits_of(count):
+    return count.bit_length() - 1
+
+
+def peer(me, rel):
+    other = me
+    for s in range(rel.bit_length()):
+        if (rel >> s) & 1:
+            step = 1 << s
+            other = other + step * (1 - 2 * lax.rem(lax.div(me, step), 2))
+    return other
+
+
+def greet(me, stages):
+    barrier = pltpu.get_barrier_semaphore()
+    for s in range(stages):
+        pl.semaphore_signal(
+            barrier, inc=1, device_id={"res": peer(me, 1 << s)}, device_id_type=MESH
+        )
+    pl.semaphore_wait(barrier, stages)
+
+
+def scatter_kernel(n, x_ref, out_ref, acc, recv, send_sem, recv_sem):
+    me = lax.axis_index("res")
+    stages = bits_of(n)
+    greet(me, stages)
+    base = [n - (n >> s) for s in range(stages)]
+
+    def copy(s, h):
+        rel = (2 * h + 1) << s
+        slot = base[s] + h
+        return pltpu.make_async_remote_copy(
+            src_ref=x_ref.at[peer(me, rel)] if s == 0 else acc.at[rel // 2],
+            dst_ref=recv.at[slot],
+            send_sem=send_sem.at[slot],
+            recv_sem=recv_sem.at[slot],
+            device_id={"res": peer(me, 1 << s)},
+            device_id_type=MESH,
+        )
+
+    def order(s):
+        names = range(n >> (s + 1))
+        return sorted(names, key=lambda h: ((h & -h) or n, -h))
+
+    copies = {}
+    for h in order(0):
+        copies[0, h] = copy(0, h)
+        copies[0, h].start()
+    rows = x_ref.shape[1]
+    part = min(rows, 128)
+    for s in range(stages):
+        for h in order(s):
+            copies[s, h].wait_recv()
+            rel = h << (s + 1)
+            slot = base[s] + h
+            source = x_ref.at[peer(me, rel)] if s == 0 else acc.at[rel // 2]
+
+            @pl.loop(0, rows // part)
+            def _(r):
+                at = pl.ds(pl.multiple_of(r * part, part), part)
+                total = source[at].astype(jnp.float32) + recv[slot, at].astype(jnp.float32)
+                if s == stages - 1:
+                    out_ref[at] = total
+                else:
+                    acc[rel // 2, at] = total.astype(jnp.bfloat16)
+
+            if h % 2 == 1:
+                copies[s + 1, h // 2] = copy(s + 1, h // 2)
+                copies[s + 1, h // 2].start()
+    for each in copies.values():
+        each.wait_send()
+
+
+def reduce_scatter(blocks):
+    n, rows, width = blocks.shape
+    return pl.pallas_call(
+        functools.partial(scatter_kernel, n),
+        out_shape=jax.ShapeDtypeStruct((rows, width), jnp.float32),
+        in_specs=[pl.BlockSpec(memory_space=pltpu.VMEM)],
+        out_specs=pl.BlockSpec(memory_space=pltpu.VMEM),
+        scratch_shapes=[
+            pltpu.VMEM((n // 2, rows, width), jnp.bfloat16),
+            pltpu.VMEM((n - 1, rows, width), jnp.bfloat16),
+            pltpu.SemaphoreType.DMA((n - 1,)),
+            pltpu.SemaphoreType.DMA((n - 1,)),
+        ],
+        compiler_params=pltpu.CompilerParams(
+            collective_id=0, has_side_effects=True, vmem_limit_bytes=VMEM_LIMIT
+        ),
+        name="reduce_scatter",
+    )(blocks)
+
+
+def gather_kernel(n, x_ref, out_ref, send_sem, recv_sem):
+    me = lax.axis_index("res")
+    stages = bits_of(n)
+    greet(me, stages)
+    base = [n - (n >> s) for s in range(stages)]
+
+    def copy(s, h):
+        owner = peer(me, h << (s + 1))
+        slot = base[s] + h
+        return pltpu.make_async_remote_copy(
+            src_ref=x_ref if h == 0 else out_ref.at[owner],
+            dst_ref=out_ref.at[owner],
+            send_sem=send_sem.at[slot],
+            recv_sem=recv_sem.at[slot],
+            device_id={"res": peer(me, 1 << s)},
+            device_id_type=MESH,
+        )
+
+    copies = {}
+
+    def pass_on(rel, stage):
+        for s in reversed(range(stage)):
+            copies[s, rel >> (s + 1)] = copy(s, rel >> (s + 1))
+            copies[s, rel >> (s + 1)].start()
+
+    pass_on(0, stages)
+    out_ref[me] = x_ref[...]
+    waits = [(s, h) for s in range(stages) for h in range(n >> (s + 1))]
+    hops = lambda s, h: bin((2 * h + 1) << s).count("1")
+    waits.sort(key=lambda sh: (hops(*sh) - stages, sh) if sh[0] >= 2 else (stages - sh[0], sh))
+    for s, h in waits:
+        copies[s, h].wait_recv()
+        pass_on((2 * h + 1) << s, s)
+    for each in copies.values():
+        each.wait_send()
+
+
+def all_gather(block, n):
+    rows, width = block.shape
+    return pl.pallas_call(
+        functools.partial(gather_kernel, n),
+        out_shape=jax.ShapeDtypeStruct((n, rows, width), block.dtype),
+        in_specs=[pl.BlockSpec(memory_space=pltpu.VMEM)],
+        out_specs=pl.BlockSpec(memory_space=pltpu.VMEM),
+        scratch_shapes=[
+            pltpu.SemaphoreType.DMA((n - 1,)),
+            pltpu.SemaphoreType.DMA((n - 1,)),
+        ],
+        compiler_params=pltpu.CompilerParams(
+            collective_id=1, has_side_effects=True, vmem_limit_bytes=VMEM_LIMIT
+        ),
+        name="all_gather",
+    )(block)
 
 
 def layer_norm(values, gain, bias):
@@ -65,12 +221,12 @@
     )
     left = left_full.astype(jnp.bfloat16)
     right = right_full.astype(jnp.bfloat16)
-    tri = lax.psum_scatter(
-        jnp.einsum("kic,kjc->jic", left, right, preferred_element_type=jnp.float32).astype(jnp.bfloat16),
-        "res",
-        scatter_dimension=0,
-        tiled=True,
-    ).astype(jnp.float32)
+    col_total, hidden = right.shape[1:]
+    axis_size = col_total // block_cols
+    share = jnp.einsum("kic,kjc->jic", left, right, preferred_element_type=jnp.float32)
+    tri = reduce_scatter(
+        share.astype(jnp.bfloat16).reshape(axis_size, block_cols * slab_rows, hidden)
+    ).reshape(block_cols, slab_rows, hidden)
     result, out_back = jax.vjp(
         lambda product, pair: output_gate(
             product, pair, norm_gain, norm_bias, tri_gain, tri_bias, weight_out, gate_out
@@ -81,7 +237,8 @@
     grad_tri, block_grad = out_back(grad_out.astype(jnp.float32))
     sent = grad_tri.astype(jnp.bfloat16)
 
-    gathered = lax.all_gather(sent, "res", axis=0, tiled=True)
+    gathered = all_gather(sent.reshape(block_cols * slab_rows, hidden), axis_size)
+    gathered = gathered.reshape(col_total, slab_rows, hidden)
     total_left = jnp.einsum("jic,kjc->kic", gathered, right, preferred_element_type=jnp.float32)
     total_right = jnp.einsum("kic,jic->kjc", left, gathered, preferred_element_type=jnp.float32)
     (grad_left,) = left_back(total_left)

time: 299 us -> 234 us (0.78)
  waiting for transfers between devices: 118 us -> 0 us
  Pallas kernels: 0 us -> 76.3 us
  between operations: 14.5 us -> 1.07 us
  matrix products: 71.4 us -> 64.8 us
    pallas_call x0 -> x2, Pallas kernels: none -> 76.3 us  [the longest x1 41.1 us: reduce_scatter(): pl.pallas_call(functools.partial(scatter_kernel, n), out_shape=jax.ShapeD...]
    reduce_scatter x1 -> x0, waiting for transfers between devices: 69.7 us -> none  [local(): lax.psum_scatter(jnp.einsum('kic,kjc->jic', left, right, preferred_elemen...]
    all_gather x1 -> x0, waiting for transfers between devices: 48.5 us -> none  [local(): gathered = lax.all_gather(sent, 'res', axis=0, tiled=True)]
    all_gather x1 -> x0, local copies, waits for them, and re-layouts: 12.9 us -> none  [local(): gathered = lax.all_gather(sent, 'res', axis=0, tiled=True)]
    dot_general x1 -> x0, local copies, waits for them, and re-layouts: 7.4 us -> none  [local(): jnp.einsum('kic,kjc->jic', left, right, preferred_element_type=jnp.float32)]
    reshape x0 -> x1, local copies, waits for them, and re-layouts: none -> 7.4 us  [local(): gathered = gathered.reshape(col_total, slab_rows, hidden)]
    convert_element_type x0 -> x1, local copies, waits for them, and re-layouts: none -> 7.36 us  [local(): share.astype(jnp.bfloat16)]
    unnamed x58 -> x48, local copies, waits for them, and re-layouts: 16.8 us -> 20.4 us
  transfers between devices with their start and end apart: 2 -> 0, of which waited for: 2 -> 0; matrix products, arithmetic and copies ran while one was open for 2% -> 0% of each run, Pallas kernels for 0% -> 0%
where the time goes in v1:
time: 234 us; the launch traced here: 233 us
  Pallas kernels  76.3 us (33%)
  matrix products  64.8 us (28%)
  local copies, waits for them, and re-layouts  61.7 us (26%)
  other arithmetic  28.6 us (12%)
    pallas_call x1, Pallas kernels, reduce_scatter(): pl.pallas_call(functools.partial(scatter_kernel, n), out_shape=jax.ShapeD...  41.1 us
    pallas_call x1, Pallas kernels, all_gather(): pl.pallas_call(functools.partial(gather_kernel, n), out_shape=jax.ShapeDt...  35.2 us
    dot_general x4, matrix products, projection(): value = jnp.dot(normed, weight, preferred_element_type=jnp.float32)  22.9 us
    unnamed x48, local copies, waits for them, and re-layouts  20.4 us
    dot_general x4, matrix products, projection(): jnp.dot(normed, gate, preferred_element_type=jnp.float32)  19.8 us
    reduce_sum x8, other arithmetic, layer_norm(): spread = jnp.mean(jnp.square(values - center), axis=-1, keepdims=True)  10.5 us
    dot_general x1, local copies, waits for them, and re-layouts, local(): jnp.einsum('kic,jic->kjc', left, gathered, preferred_element_type=jnp.flo...  9.28 us
    convert_element_type x3, other arithmetic, layer_norm(): values = values.astype(jnp.float32)  9.2 us

profile of v1, /device:TPU:11, one launch (start us, length us, event | category | flops | bytes accessed | tf_op | source)
XLA Modules:
  0.0 232.6 jit_solution(17860299374875500197)
XLA Ops:
  0.7 0.8 broadcast_in_dim.12
  1.6 0.7 broadcast_in_dim.13
  2.4 1.2 convert_reduce_fusion.2
  3.6 1.3 fusion.74
  4.9 0.7 maximum_convert_fusion.1
  5.7 1.8 convert_reduce_fusion.1
  7.5 2.3 %fusion.33 = f32[64,64]{1,0:T(8,128)S(1)} fusion(bf16[64,64,128]{2,1,0:T(8,128)(2,1)} %param.19, f32[64,64]{1,0:T(8,128)S(1)} %broadcast_multiply_fusion.1), kind=kLoop, calls=%fused_computation.44 | loop fusion | flops 2093056 | bytes 1081344 | tf_op jit(solution)/shard_map/jvp()/reduce_sum | solution.py:166
  9.9 0.8 maximum_convert_fusion
  10.7 1.4 fusion.54
  12.2 1.3 add_divide_fusion.1
  13.5 1.3 copy-done.11
  14.8 3.2 %multiply_convert_fusion.1 = (bf16[64,64,128]{2,1,0:T(8,128)(2,1)S(1)}, f32[64,64,128]{2,1,0:T(8,128)}) fusion(f32[64,64,128]{2,1,0:T(8,128)S(1)} %add_divide_fusion.1, f32[64,64]{1,0:T(8,128)S(1)} %maximum_convert_fusion.1, bf16[128,128]{1,0:T(8,128)(2,1)S(1)} %copy-done.15, bf16[64,64,128]{2,1,0:T(8,128)(2,1)S(1)} %copy-done.8, f32[128]{0:T(128)S(1)} %copy-done.20, ...), kind=kOutput, calls=%fused_computation.58 | convolution fusion | flops 138936320 | bytes 6374400 | tf_op jit(solution)/shard_map/jvp()/dot_general | solution.py:172
  18.0 3.7 %copy.32 = bf16[64,64,128]{1,0,2:T(8,128)(2,1)} copy(bf16[64,64,128]{2,1,0:T(8,128)(2,1)S(1)} %get-tuple-element.16) | data formatting | bytes 2097152 | tf_op jit(solution)/shard_map/convert_element_type | solution.py:222
  21.7 6.4 %copy.22 = bf16[64,256,128]{1,2,0:T(8,128)(2,1)} copy(bf16[64,256,128]{2,1,0:T(8,128)(2,1)} %param.20) | data formatting | bytes 8388608 | tf_op args[1]
  28.1 3.4 %convert_reduce_fusion = f32[64,256]{1,0:T(8,128)S(1)} fusion(bf16[64,256,128]{1,2,0:T(8,128)(2,1)} %copy.22), kind=kLoop, calls=%fused_computation.2 | loop fusion | flops 4177920 | bytes 4259840 | tf_op jit(solution)/shard_map/jvp()/reduce_sum | solution.py:165
  31.5 1.6 fusion.8
  33.2 2.9 %add_divide_fusion = f32[64,256,128]{2,1,0:T(8,128)S(1)} fusion(bf16[128,128]{1,0:T(8,128)(2,1)S(1)} %copy-done.18, bf16[64,256,128]{1,2,0:T(8,128)(2,1)S(1)} %copy-done.3, f32[128]{0:T(128)S(1)} %copy-done.20, f32[128]{0:T(128)S(1)} %copy-done.19, f32[64,256]{1,0:T(8,128)S(1)} %fusion.96, f32[64,256]{1,0:T(8,128)S(1)} %broadcast_multiply_fusion), kind=kOutput, calls=%fused_computation.26 | convolution fusion | flops 555745280 | bytes 12747776 | tf_op jit(solution)/shard_map/jvp()/dot_general | solution.py:173
  36.1 7.3 %multiply_convert_fusion = (bf16[64,256,128]{2,1,0:T(8,128)(2,1)}, f32[64,256,128]{2,1,0:T(8,128)}) fusion(f32[64,256,128]{2,1,0:T(8,128)S(1)} %add_divide_fusion, f32[64,256]{1,0:T(8,128)S(1)} %maximum_convert_fusion, bf16[128,128]{1,0:T(8,128)(2,1)S(1)} %copy-done, bf16[64,256,128]{1,2,0:T(8,128)(2,1)S(1)} %copy-done.3, f32[128]{0:T(128)S(1)} %copy-done.20, ...), kind=kOutput, calls=%fused_computation.25 | convolution fusion | flops 555745280 | bytes 25396224 | tf_op jit(solution)/shard_map/jvp()/dot_general | solution.py:172
  43.5 6.8 %copy.28 = bf16[64,256,128]{1,0,2:T(8,128)(2,1)} copy(bf16[64,256,128]{2,1,0:T(8,128)(2,1)} %get-tuple-element.14) | data formatting | bytes 8388608 | tf_op jit(solution)/shard_map/convert_element_type | solution.py:223
  50.3 6.1 %convert_bitcast_fusion = bf16[256,64,128]{0,1,2:T(8,128)(2,1)} fusion(bf16[64,64,128]{1,0,2:T(8,128)(2,1)} %copy.32, bf16[64,256,128]{1,0,2:T(8,128)(2,1)} %copy.28), kind=kOutput, calls=%fused_computation.29 | convolution fusion | flops 270532608 | bytes 9437184 | tf_op jit(solution)/shard_map/kic,kjc->jic/dot_general | solution.py:226
  56.3 7.4 %copy.27 = bf16[256,64,128]{2,1,0:T(8,128)(2,1)} copy(bf16[256,64,128]{0,1,2:T(8,128)(2,1)} %convert_bitcast_fusion) | data formatting | bytes 8388608 | tf_op jit(solution)/shard_map/convert_element_type | solution.py:228
  63.7 2.2 copy-done.1
  65.9 41.1 %reduce_scatter.1 = f32[1024,128]{1,0:T(8,128)S(1)} custom-call(bf16[16,1024,128]{2,1,0:T(8,128)(2,1)S(1)} %bitcast.92), custom_call_target="tpu_custom_call" | custom-call | tf_op jit(solution)/shard_map/reduce_scatter/pallas_call | solution.py:90
  107.3 0.4 multiply_reduce_fusion.2
  107.8 1.9 multiply_reduce_fusion.3
  109.7 0.5 fusion.70
  110.3 1.3 fusion.73
  111.6 1.6 multiply_reduce_fusion.4
  113.3 0.5 multiply_reduce_fusion
  113.9 0.6 add_convert_fusion.1
  114.5 35.2 %all_gather.1 = bf16[16,1024,128]{2,1,0:T(8,128)(2,1)S(1)} custom-call(bf16[1024,128]{1,0:T(8,128)(2,1)S(1)} %bitcast.94), custom_call_target="tpu_custom_call" | custom-call | tf_op jit(solution)/shard_map/all_gather/pallas_call | solution.py:147
  149.7 2.0 copy-done.2
  151.7 7.4 %copy.29 = bf16[256,64,128]{0,1,2:T(8,128)(2,1)} copy(bf16[256,64,128]{2,1,0:T(8,128)(2,1)} %bitcast.93) | data formatting | bytes 8388608 | tf_op jit(solution)/shard_map/reshape | solution.py:241
  159.1 6.7 %fusion.123 = f32[128,64,64]{2,1,0:T(8,128)} fusion(bf16[64,256,128]{1,0,2:T(8,128)(2,1)} %copy.28, bf16[256,64,128]{0,1,2:T(8,128)(2,1)} %copy.29), kind=kOutput, calls=%fused_computation.156 | convolution fusion | flops 268435456 | bytes 10485760 | tf_op jit(solution)/shard_map/jic,kjc->kic/dot_general | solution.py:242
  165.8 4.8 %copy.30 = f32[128,64,64]{0,2,1:T(8,128)} copy(f32[128,64,64]{2,1,0:T(8,128)} %fusion.123) | data formatting | bytes 4194304 | tf_op jit(solution)/shard_map/jic,kjc->kic/dot_general | solution.py:242
  170.6 3.7 %fusion.47 = bf16[64,64,128]{2,1,0:T(8,128)(2,1)S(1)} fusion(f32[64,64,128]{2,1,0:T(8,128)} %copy-done.11, f32[64,64,128]{2,1,0:T(8,128)} %get-tuple-element.17, f32[128,64,64]{0,2,1:T(8,128)} %copy.30, f32[64,64]{1,0:T(8,128)S(1)} %maximum_convert_fusion.1, bf16[128,128]{1,0:T(8,128)(2,1)S(1)} %copy-done.17), kind=kOutput, calls=%fused_computation.61 | convolution fusion | flops 137363456 | bytes 7389184 | tf_op jit(solution)/shard_map/transpose(jvp())/dot_general | solution.py:173
  174.3 0.3 copy-done.12
  174.7 3.1 %fusion.45 = (f32[64,64]{1,0:T(8,128)S(1)}, f32[64,64]{1,0:T(8,128)S(1)}, bf16[64,64,128]{2,1,0:T(8,128)(2,1)S(1)}) fusion(f32[128]{0:T(128)S(1)} %copy-done.19, f32[64,64]{1,0:T(8,128)S(1)} %fusion.111, f32[64,64]{1,0:T(8,128)S(1)} %broadcast_multiply_fusion.1, bf16[64,64,128]{2,1,0:T(8,128)(2,1)S(1)} %copy-done.8, bf16[64,64,128]{2,1,0:T(8,128)(2,1)S(1)} %fusion.47, ...), kind=kOutput, calls=%fused_computation.57 | convolution fusion | flops 140500992 | bytes 7455232 | tf_op jit(solution)/shard_map/transpose(jvp())/dot_general | solution.py:172
  177.9 1.8 fusion.29
  179.7 3.5 %fusion.32 = bf16[64,64,128]{2,1,0:T(8,128)(2,1)} fusion(bf16[64,64,128]{2,1,0:T(8,128)(2,1)S(1)} %copy-done.8, bf16[64,64,128]{2,1,0:T(8,128)(2,1)S(1)} %get-tuple-element.19, f32[64,64]{1,0:T(8,128)S(1)} %add_multiply_fusion.1, f32[64,64]{1,0:T(8,128)S(1)} %multiply_multiply_fusion.1, f32[128]{0:T(128)S(1)} %copy-done.19, f32[64,64]{1,0:T(8,128)S(1)} %fusion.111, ...), kind=kLoop, calls=%fused_computation.43 | loop fusion | flops 4718592 | bytes 3211776 | tf_op jit(solution)/shard_map/transpose(jvp())/convert_element_type | solution.py:164
  183.2 4.4 %fusion.124 = f32[128,256,64]{1,2,0:T(8,128)} fusion(bf16[64,64,128]{1,0,2:T(8,128)(2,1)S(1)} %copy-done.9, bf16[256,64,128]{0,1,2:T(8,128)(2,1)S(1)} %copy-done.7), kind=kOutput, calls=%fused_computation.157 | convolution fusion | flops 268435456 | bytes 13631488 | tf_op jit(solution)/shard_map/kic,jic->kjc/dot_general | solution.py:243
  187.6 9.3 %copy.33 = f32[128,256,64]{0,1,2:T(8,128)} copy(f32[128,256,64]{1,2,0:T(8,128)} %fusion.124) | data formatting | bytes 16777216 | tf_op jit(solution)/shard_map/kic,jic->kjc/dot_general | solution.py:243
  196.9 11.9 %fusion.14 = bf16[64,256,128]{1,2,0:T(8,128)(2,1)} fusion(f32[64,256,128]{2,1,0:T(8,128)} %copy-done.5, f32[64,256,128]{2,1,0:T(8,128)} %get-tuple-element.15, f32[128,256,64]{0,1,2:T(8,128)} %copy.33, f32[64,256]{1,0:T(8,128)S(1)} %maximum_convert_fusion, bf16[128,128]{1,0:T(8,128)(2,1)S(1)} %copy-done.18), kind=kOutput, calls=%fused_computation.17 | convolution fusion | flops 547356672 | bytes 29458432 | tf_op jit(solution)/shard_map/transpose(jvp())/dot_general | solution.py:173
  208.8 1.5 copy-done.6
  210.3 9.3 %fusion.20 = (f32[64,256]{1,0:T(8,128)S(1)}, f32[64,256]{1,0:T(8,128)S(1)}, bf16[64,256,128]{1,2,0:T(8,128)(2,1)}) fusion(f32[128]{0:T(128)S(1)} %copy-done.19, f32[64,256]{1,0:T(8,128)S(1)} %fusion.96, f32[64,256]{1,0:T(8,128)S(1)} %broadcast_multiply_fusion, bf16[64,256,128]{1,2,0:T(8,128)(2,1)S(1)} %copy-done.4, bf16[64,256,128]{1,2,0:T(8,128)(2,1)} %fusion.14, ...), kind=kOutput, calls=%fused_computation.24 | convolution fusion | flops 562003968 | bytes 29721088 | tf_op jit(solution)/shard_map/transpose(jvp())/dot_general | solution.py:172
  219.7 2.0 fusion.4
  221.8 4.4 %fusion.7 = bf16[64,256,128]{1,2,0:T(8,128)(2,1)} fusion(bf16[64,256,128]{1,2,0:T(8,128)(2,1)S(1)} %copy-done.4, bf16[64,256,128]{1,2,0:T(8,128)(2,1)S(1)} %copy-done.13, f32[64,256]{1,0:T(8,128)S(1)} %add_multiply_fusion, f32[64,256]{1,0:T(8,128)S(1)} %multiply_multiply_fusion, f32[128]{0:T(128)S(1)} %copy-done.19, f32[64,256]{1,0:T(8,128)S(1)} %fusion.96, ...), kind=kLoop, calls=%fused_computation.10 | loop fusion | flops 18874368 | bytes 12845568 | tf_op jit(solution)/shard_map/transpose(jvp())/convert_element_type | solution.py:164
  226.2 6.4 %copy.34 = bf16[64,256,128]{2,1,0:T(8,128)(2,1)} copy(bf16[64,256,128]{1,2,0:T(8,128)(2,1)} %fusion.7) | data formatting | bytes 8388608
  (66 shorter events, 1.1 us)
Async XLA Ops:
  0.6 35.5 %copy-start = (bf16[128,128]{1,0:T(8,128)(2,1)S(1)}, bf16[128,128]{1,0:T(8,128)(2,1)}, u32[]{:S(2)}) copy-start(bf16[128,128]{1,0:T(8,128)(2,1)} %param.27) | copy-start | bytes 98308
  0.6 11.5 %copy-start.19 = (f32[128]{0:T(128)S(1)}, f32[128]{0:T(128)}, u32[]{:S(2)}) copy-start(f32[128]{0:T(128)} %param.23) | copy-start | bytes 1540
  0.7 11.5 %copy-start.8 = (bf16[64,64,128]{2,1,0:T(8,128)(2,1)S(1)}, bf16[64,64,128]{2,1,0:T(8,128)(2,1)}, u32[]{:S(2)}) copy-start(bf16[64,64,128]{2,1,0:T(8,128)(2,1)} %param.19) | copy-start | bytes 3145732
  0.7 11.5 %copy-start.20 = (f32[128]{0:T(128)S(1)}, f32[128]{0:T(128)}, u32[]{:S(2)}) copy-start(f32[128]{0:T(128)} %param.24) | copy-start | bytes 1540
  0.7 11.5 %copy-start.17 = (bf16[128,128]{1,0:T(8,128)(2,1)S(1)}, bf16[128,128]{1,0:T(8,128)(2,1)}, u32[]{:S(2)}) copy-start(bf16[128,128]{1,0:T(8,128)(2,1)} %param.26) | copy-start | bytes 98308
  12.2 2.7 %copy-start.15 = (bf16[128,128]{1,0:T(8,128)(2,1)S(1)}, bf16[128,128]{1,0:T(8,128)(2,1)}, u32[]{:S(2)}) copy-start(bf16[128,128]{1,0:T(8,128)(2,1)} %param.25) | copy-start | bytes 98308
  13.5 1.4 copy-start.11
  28.1 3.4 %copy-start.3 = (bf16[64,256,128]{1,2,0:T(8,128)(2,1)S(1)}, bf16[64,256,128]{1,2,0:T(8,128)(2,1)}, u32[]{:S(2)}) copy-start(bf16[64,256,128]{1,2,0:T(8,128)(2,1)} %copy.22) | copy-start | bytes 12582916
  28.1 5.1 %copy-start.18 = (bf16[128,128]{1,0:T(8,128)(2,1)S(1)}, bf16[128,128]{1,0:T(8,128)(2,1)}, u32[]{:S(2)}) copy-start(bf16[128,128]{1,0:T(8,128)(2,1)} %param.28) | copy-start | bytes 98308
  36.1 7.3 %copy-start.5 = (f32[64,256,128]{2,1,0:T(8,128)}, f32[64,256,128]{2,1,0:T(8,128)S(1)}, u32[]{:S(2)}) copy-start(f32[64,256,128]{2,1,0:T(8,128)S(1)} %add_divide_fusion) | copy-start | bytes 25165828
  63.7 44.1 %copy-start.21 = (f32[128]{0:T(128)S(1)}, f32[128]{0:T(128)}, u32[]{:S(2)}) copy-start(f32[128]{0:T(128)} %param.29) | copy-start | bytes 1540
  63.7 44.1 %copy-start.22 = (f32[128]{0:T(128)S(1)}, f32[128]{0:T(128)}, u32[]{:S(2)}) copy-start(f32[128]{0:T(128)} %param.30) | copy-start | bytes 1540
  63.7 2.2 copy-start.1
  65.9 41.9 %copy-start.14 = (bf16[16,64,128]{2,1,0:T(8,128)(2,1)S(1)}, bf16[16,64,128]{2,1,0:T(8,128)(2,1)}, u32[]{:S(2)}) copy-start(bf16[16,64,128]{2,1,0:T(8,128)(2,1)} %param.21) | copy-start | bytes 786436
  65.9 41.9 %copy-start.16 = (bf16[128,128]{1,0:T(8,128)(2,1)S(1)}, bf16[128,128]{1,0:T(8,128)(2,1)}, u32[]{:S(2)}) copy-start(bf16[128,128]{1,0:T(8,128)(2,1)} %param.31) | copy-start | bytes 98308
  149.7 2.0 copy-start.2
  170.6 3.7 %copy-start.10 = (f32[128,64,64]{0,2,1:T(8,128)S(1)}, f32[128,64,64]{0,2,1:T(8,128)}, u32[]{:S(2)}) copy-start(f32[128,64,64]{0,2,1:T(8,128)} %copy.30) | copy-start | bytes 6291460
  170.6 4.1 %copy-start.12 = (f32[64,64,128]{2,1,0:T(8,128)S(1)}, f32[64,64,128]{2,1,0:T(8,128)}, u32[]{:S(2)}) copy-start(f32[64,64,128]{2,1,0:T(8,128)} %copy-done.11) | copy-start | bytes 6291460
  174.7 8.5 %copy-start.9 = (bf16[64,64,128]{1,0,2:T(8,128)(2,1)S(1)}, bf16[64,64,128]{1,0,2:T(8,128)(2,1)}, u32[]{:S(2)}) copy-start(bf16[64,64,128]{1,0,2:T(8,128)(2,1)} %copy.32) | copy-start | bytes 3145732
  177.8 5.4 %copy-start.7 = (bf16[256,64,128]{0,1,2:T(8,128)(2,1)S(1)}, bf16[256,64,128]{0,1,2:T(8,128)(2,1)}, u32[]{:S(2)}) copy-start(bf16[256,64,128]{0,1,2:T(8,128)(2,1)} %copy.29) | copy-start | bytes 12582916
  196.9 11.9 %copy-start.4 = (bf16[64,256,128]{1,2,0:T(8,128)(2,1)S(1)}, bf16[64,256,128]{1,2,0:T(8,128)(2,1)}, u32[]{:S(2)}) copy-start(bf16[64,256,128]{1,2,0:T(8,128)(2,1)} %copy.22) | copy-start | bytes 12582916
  196.9 13.4 %copy-start.6 = (f32[128,256,64]{0,1,2:T(8,128)S(1)}, f32[128,256,64]{0,1,2:T(8,128)}, u32[]{:S(2)}) copy-start(f32[128,256,64]{0,1,2:T(8,128)} %copy.33) | copy-start | bytes 25165828
  219.6 2.2 copy-start.13

commit v2 on v1

--- a/solution.py
+++ b/solution.py
@@ -160,18 +160,92 @@
     )(block)
 
 
+def masked(shape, first, rows_ref, tile_ref, chain_ref):
+    count = shape[0] // chain_ref.shape[0]
+    parts = [(chain_ref[...] == rows_ref[0, first + m]) | (tile_ref[...] > 0) for m in range(count)]
+    return parts[0] if count == 1 else jnp.concatenate(parts, axis=0)
+
+
+def normed_parts(pair, gain, bias):
+    values = pair.astype(jnp.float32)
+    center = jnp.mean(values, axis=-1, keepdims=True)
+    values = values - center
+    scale = lax.rsqrt(jnp.mean(values * values, axis=-1, keepdims=True) + 1e-05)
+    unit = values * scale
+    return unit, scale, (unit * gain + bias).astype(jnp.bfloat16)
+
+
+def gated(normed, both_ref):
+    hidden = both_ref.shape[1] // 2
+    products = jnp.dot(normed, both_ref[...], preferred_element_type=jnp.float32)
+    return products[:, :hidden], 0.5 * jnp.tanh(0.5 * products[:, hidden:]) + 0.5
+
+
+def forward_kernel(rows_ref, pair_ref, gain_ref, bias_ref, both_ref, tile_ref, chain_ref, out_ref):
+    inner = chain_ref.shape[0]
+    step = max(inner, min(256, pair_ref.shape[0]))
+    ratio = step // inner
+    start = pl.program_id(0) * (pair_ref.shape[0] // inner)
+
+    @pl.loop(0, pair_ref.shape[0] // step)
+    def _(t):
+        at = pl.ds(pl.multiple_of(t * step, step), step)
+        unused, unused, normed = normed_parts(pair_ref[at], gain_ref[...], bias_ref[...])
+        value, gating = gated(normed, both_ref)
+        keep = masked((step,), start + t * ratio, rows_ref, tile_ref, chain_ref)
+        out_ref[at] = jnp.where(keep, gating * value, 0.0).astype(jnp.bfloat16)
+
+
+def backward_kernel(
+    rows_ref, pair_ref, grad_ref, gain_ref, bias_ref, both_ref, back_ref, tile_ref, chain_ref, out_ref
+):
+    inner = chain_ref.shape[0]
+    step = max(inner, min(256, pair_ref.shape[0]))
+    ratio = step // inner
+    start = pl.program_id(0) * (pair_ref.shape[0] // inner)
+
+    @pl.loop(0, pair_ref.shape[0] // step)
+    def _(t):
+        at = pl.ds(pl.multiple_of(t * step, step), step)
+        gain = gain_ref[...]
+        unit, scale, normed = normed_parts(pair_ref[at], gain, bias_ref[...])
+        value, gating = gated(normed, both_ref)
+        keep = masked((step,), start + t * ratio, rows_ref, tile_ref, chain_ref)
+        grad = jnp.where(keep, grad_ref[at].astype(jnp.float32), 0.0)
+        grad_value = grad * gating
+        grad_gate = grad_value * value * (1.0 - gating)
+        pulled = jnp.concatenate(
+            [grad_value.astype(jnp.bfloat16), grad_gate.astype(jnp.bfloat16)], axis=1
+        )
+        grad_normed = jnp.dot(pulled, back_ref[...], preferred_element_type=jnp.float32)
+        grad_unit = grad_normed.astype(jnp.bfloat16).astype(jnp.float32) * gain
+        mean_grad = jnp.mean(grad_unit, axis=-1, keepdims=True)
+        mean_dot = jnp.mean(grad_unit * unit, axis=-1, keepdims=True)
+        out_ref[at] = (scale * (grad_unit - mean_grad - unit * mean_dot)).astype(jnp.bfloat16)
+
+
+def per_row(kernel, name, streamed, fixed, chain_rows, inner, width):
+    rows = streamed[0].shape[0]
+    block = min(rows, 2048)
+    whole = lambda array: pl.BlockSpec(array.shape, lambda g: (0, 0))
+    return pl.pallas_call(
+        kernel,
+        grid=(rows // block,),
+        out_shape=jax.ShapeDtypeStruct((rows, width), jnp.bfloat16),
+        in_specs=[pl.BlockSpec(memory_space=pltpu.SMEM)]
+        + [pl.BlockSpec((block, each.shape[1]), lambda g: (g, 0)) for each in streamed]
+        + [whole(each) for each in fixed],
+        out_specs=pl.BlockSpec((block, width), lambda g: (g, 0)),
+        compiler_params=pltpu.CompilerParams(vmem_limit_bytes=VMEM_LIMIT),
+        name=name,
+    )(chain_rows[None, :], *streamed, *fixed)
+
+
 def layer_norm(values, gain, bias):
     values = values.astype(jnp.float32)
     center = jnp.mean(values, axis=-1, keepdims=True)
     spread = jnp.mean(jnp.square(values - center), axis=-1, keepdims=True)
     return (values - center) * lax.rsqrt(spread + 1e-05) * gain + bias
-
-
-def projection(pair, mask, norm_gain, norm_bias, weight, gate):
-    normed = layer_norm(pair, norm_gain, norm_bias).astype(jnp.bfloat16)
-    value = jnp.dot(normed, weight, preferred_element_type=jnp.float32)
-    gating = jax.nn.sigmoid(jnp.dot(normed, gate, preferred_element_type=jnp.float32))
-    return mask[..., None] * gating * value
 
 
 def output_gate(tri, pair, norm_gain, norm_bias, tri_gain, tri_bias, weight_out, gate_out):
@@ -205,23 +279,26 @@
     slab_rows = pair_left.shape[1]
     block_cols = pair_block.shape[0]
     tile_rows = slab_rows // tile_left.shape[1]
-    same_left = (chain_rows[:, None] == chain_slab[None, :]).astype(jnp.int32)
-    mask_left = jnp.maximum(jnp.repeat(tile_left, tile_rows, axis=1), same_left).astype(jnp.float32)
-    same_right = (chain_rows[:, None] == chain_cols[None, :]).astype(jnp.int32)
-    mask_right = jnp.maximum(jnp.repeat(tile_right, block_cols, axis=1), same_right).astype(
-        jnp.float32
-    )
-    left_full, left_back = jax.vjp(
-        lambda pair: projection(pair, mask_left, norm_gain, norm_bias, weight_left, gate_left),
-        pair_left,
-    )
-    right_full, right_back = jax.vjp(
-        lambda pair: projection(pair, mask_right, norm_gain, norm_bias, weight_right, gate_right),
-        pair_right,
-    )
-    left = left_full.astype(jnp.bfloat16)
-    right = right_full.astype(jnp.bfloat16)
-    col_total, hidden = right.shape[1:]
+    row_total, unused, channels = pair_left.shape
+    col_total = pair_right.shape[1]
+    hidden = weight_left.shape[1]
+    gain, bias = norm_gain[None, :], norm_bias[None, :]
+    spread = lambda line: jnp.broadcast_to(line[:, None], (line.shape[0], hidden))
+    tiles_left = spread(jnp.repeat(tile_left[0], tile_rows))
+    tiles_right = spread(jnp.repeat(tile_right[0], block_cols))
+    chains_left, chains_right = spread(chain_slab), spread(chain_cols)
+    both_left = jnp.concatenate([weight_left, gate_left], axis=1)
+    both_right = jnp.concatenate([weight_right, gate_right], axis=1)
+    rows_left = pair_left.reshape(row_total * slab_rows, channels)
+    rows_right = pair_right.reshape(row_total * col_total, channels)
+    left = per_row(
+        forward_kernel, "left_forward", [rows_left],
+        [gain, bias, both_left, tiles_left, chains_left], chain_rows, slab_rows, hidden,
+    ).reshape(row_total, slab_rows, hidden)
+    right = per_row(
+        forward_kernel, "right_forward", [rows_right],
+        [gain, bias, both_right, tiles_right, chains_right], chain_rows, col_total, hidden,
+    ).reshape(row_total, col_total, hidden)
     axis_size = col_total // block_cols
     share = jnp.einsum("kic,kjc->jic", left, right, preferred_element_type=jnp.float32)
     tri = reduce_scatter(
@@ -241,8 +318,18 @@
     gathered = gathered.reshape(col_total, slab_rows, hidden)
     total_left = jnp.einsum("jic,kjc->kic", gathered, right, preferred_element_type=jnp.float32)
     total_right = jnp.einsum("kic,jic->kjc", left, gathered, preferred_element_type=jnp.float32)
-    (grad_left,) = left_back(total_left)
-    (grad_right,) = right_back(total_right)
+    grad_left = per_row(
+        backward_kernel, "left_backward",
+        [rows_left, total_left.astype(jnp.bfloat16).reshape(row_total * slab_rows, hidden)],
+        [gain, bias, both_left, both_left.T, tiles_left, chains_left],
+        chain_rows, slab_rows, channels,
+    ).reshape(pair_left.shape)
+    grad_right = per_row(
+        backward_kernel, "right_backward",
+        [rows_right, total_right.astype(jnp.bfloat16).reshape(row_total * col_total, hidden)],
+        [gain, bias, both_right, both_right.T, tiles_right, chains_right],
+        chain_rows, col_total, channels,
+    ).reshape(pair_right.shape)
     return (grad_left, grad_right, block_grad)
 
 

time: 234 us -> 243 us (1.038)
  Pallas kernels: 76.3 us -> 157 us
  matrix products: 64.8 us -> 21.1 us
  other arithmetic: 28.6 us -> 9.58 us
  local copies, waits for them, and re-layouts: 61.7 us -> 52.5 us
    pallas_call x0 -> x4, Pallas kernels: none -> 81 us  [per_row(): pl.pallas_call(kernel, grid=(rows // block,), out_shape=jax.ShapeDtypeStr...]
    dot_general x8 -> x0, matrix products: 42.7 us -> none  [the longest x4 22.9 us: projection(): value = jnp.dot(normed, weight, preferred_element_type=jnp.float32)]
    dot_general x2 -> x0, local copies, waits for them, and re-layouts: 14.1 us -> none  [the longest x1 9.28 us: local(): jnp.einsum('kic,jic->kjc', left, gathered, preferred_element_type=jnp.flo...]
    reshape x0 -> x2, local copies, waits for them, and re-layouts: none -> 10.5 us  [the longest x1 6.8 us: local(): right = per_row(forward_kernel, 'right_forward', [rows_right], [gain, bia...]
    reduce_sum x8 -> x4, other arithmetic: 10.5 us -> 2.72 us  [layer_norm(): spread = jnp.mean(jnp.square(values - center), axis=-1, keepdims=True)]
    unnamed x48 -> x34, local copies, waits for them, and re-layouts: 20.4 us -> 13.1 us
    convert_element_type x3 -> x1, other arithmetic: 9.2 us -> 2.02 us  [layer_norm(): values = values.astype(jnp.float32)]
    reduce_sum x4 -> x2, other arithmetic: 6.57 us -> 1.37 us  [layer_norm(): center = jnp.mean(values, axis=-1, keepdims=True)]
where the time goes in v2:
time: 243 us; the launch traced here: 242 us
  Pallas kernels  157 us (65%)
  local copies, waits for them, and re-layouts  52.5 us (22%)
  matrix products  21.1 us (9%)
  other arithmetic  9.58 us (4%)
    pallas_call x4, Pallas kernels, per_row(): pl.pallas_call(kernel, grid=(rows // block,), out_shape=jax.ShapeDtypeStr...  81 us
    pallas_call x1, Pallas kernels, reduce_scatter(): pl.pallas_call(functools.partial(scatter_kernel, n), out_shape=jax.ShapeD...  41.1 us
    pallas_call x1, Pallas kernels, all_gather(): pl.pallas_call(functools.partial(gather_kernel, n), out_shape=jax.ShapeDt...  35.2 us
    unnamed x34, local copies, waits for them, and re-layouts  13.1 us
    reshape x1, local copies, waits for them, and re-layouts, local(): gathered = gathered.reshape(col_total, slab_rows, hidden)  7.43 us
    convert_element_type x1, local copies, waits for them, and re-layouts, local(): share.astype(jnp.bfloat16)  7.37 us
    convert_element_type x1, local copies, waits for them, and re-layouts, local(): total_right.astype(jnp.bfloat16).reshape(row_total * col_total, hidden)  6.87 us
    reshape x1, local copies, waits for them, and re-layouts, local(): right = per_row(forward_kernel, 'right_forward', [rows_right], [gain, bia...  6.8 us

profile of v2, /device:TPU:11, one launch (start us, length us, event | category | flops | bytes accessed | tf_op | source)
XLA Modules:
  0.0 241.5 jit_solution(16936862130951770877)
XLA Ops:
  0.7 0.8 broadcast_in_dim.33
  1.5 0.1 broadcast_in_dim.68
  1.6 0.7 broadcast_in_dim.29
  2.4 1.2 convert_reduce_fusion
  3.6 1.3 fusion.19
  5.0 0.7 broadcast_in_dim.70.chain_ref
  5.7 0.9 copy.25
  6.6 0.9 copy.26
  7.5 0.9 copy.22
  8.4 0.9 copy.23
  9.3 0.1 copy.24.both_ref
  9.4 0.1 copy.27.both_ref
  9.5 0.1 broadcast_in_dim.31.tile_ref
  9.6 0.8 broadcast_in_dim.32.chain_ref
  10.4 1.4 fusion.2
  11.9 6.0 %left_forward.1 = bf16[4096,128]{1,0:T(8,128)(2,1)S(1)} custom-call(s32[1,64]{1,0:T(1,128)S(1)} %bitcast.63, bf16[4096,128]{1,0:T(8,128)(2,1)S(1)} %bitcast.60, f32[1,128]{1,0:T(1,128)S(1)} %bitcast.67, f32[1,128]{1,0:T(1,128)S(1)} %bitcast.71, bf16[128,256]{1,0:T(8,128)(2,1)S(1)} %copy.27.both_ref, s32[64,128]{1,0:T(8,128)S(1)} %broadcast_in_dim.69.tile_ref, ...), custom_call_target="tpu_custom_call" | custom-call | tf_op jit(solution)/shard_map/left_forward/pallas_call | solution.py:231
  17.9 3.8 %copy.36 = bf16[64,64,128]{1,0,2:T(8,128)(2,1)} copy(bf16[64,64,128]{2,1,0:T(8,128)(2,1)S(1)} %bitcast.58) | data formatting | bytes 2097152 | tf_op jit(solution)/shard_map/reshape | solution.py:297
  21.7 23.1 %right_forward.1 = bf16[16384,128]{1,0:T(8,128)(2,1)S(1)} custom-call(s32[1,64]{1,0:T(1,128)S(1)} %bitcast.64, bf16[16384,128]{1,0:T(8,128)(2,1)} %bitcast.56, f32[1,128]{1,0:T(1,128)S(1)} %bitcast.68, f32[1,128]{1,0:T(1,128)S(1)} %bitcast.72, bf16[128,256]{1,0:T(8,128)(2,1)S(1)} %copy.24.both_ref, s32[256,128]{1,0:T(8,128)S(1)} %broadcast_in_dim.31.tile_ref, ...), custom_call_target="tpu_custom_call" | custom-call | tf_op jit(solution)/shard_map/right_forward/pallas_call | solution.py:231
  44.8 2.0 copy-done.1
  46.8 6.8 %copy.31 = bf16[64,256,128]{1,0,2:T(8,128)(2,1)} copy(bf16[64,256,128]{2,1,0:T(8,128)(2,1)} %bitcast.53) | data formatting | bytes 8388608 | tf_op jit(solution)/shard_map/reshape | solution.py:301
  53.6 6.1 %convert_bitcast_fusion.1 = bf16[256,64,128]{0,1,2:T(8,128)(2,1)} fusion(bf16[64,64,128]{1,0,2:T(8,128)(2,1)} %copy.36, bf16[64,256,128]{1,0,2:T(8,128)(2,1)} %copy.31), kind=kOutput, calls=%fused_computation.1 | convolution fusion | flops 270532608 | bytes 9437184 | tf_op jit(solution)/shard_map/kic,kjc->jic/dot_general | solution.py:303
  59.7 7.4 %copy.30 = bf16[256,64,128]{2,1,0:T(8,128)(2,1)} copy(bf16[256,64,128]{0,1,2:T(8,128)(2,1)} %convert_bitcast_fusion.1) | data formatting | bytes 8388608 | tf_op jit(solution)/shard_map/convert_element_type | solution.py:305
  67.1 2.2 copy-done.2
  69.3 41.1 %reduce_scatter.1 = f32[1024,128]{1,0:T(8,128)S(1)} custom-call(bf16[16,1024,128]{2,1,0:T(8,128)(2,1)S(1)} %bitcast.54), custom_call_target="tpu_custom_call" | custom-call | tf_op jit(solution)/shard_map/reduce_scatter/pallas_call | solution.py:90
  110.4 0.2 reduce_sum.93
  110.6 0.4 multiply_reduce_fusion.2
  111.0 0.6 copy-done.13
  111.7 0.6 copy-done.12
  112.3 2.5 %multiply_reduce_fusion.3 = (f32[16,64]{1,0:T(8,128)}, f32[16,64]{1,0:T(8,128)}, f32[16,64,128]{2,1,0:T(8,128)S(1)}) fusion(f32[16,64]{1,0:T(8,128)} %copy-done.14, f32[16,64]{1,0:T(8,128)S(1)} %broadcast_multiply_fusion, bf16[16,64,128]{2,1,0:T(8,128)(2,1)S(1)} %copy-done.11, f32[128]{0:T(128)S(1)} %copy-done.7, bf16[128,128]{1,0:T(8,128)(2,1)} %param.32, ...), kind=kOutput, calls=%fused_computation.39 | convolution fusion | flops 69597184 | bytes 2188800 | tf_op jit(solution)/shard_map/transpose(jvp())/dot_general | solution.py:253
  114.9 0.7 multiply_multiply_fusion
  115.6 0.5 fusion.15
  116.1 0.7 add_multiply_fusion
  116.8 2.0 fusion.18
  118.8 1.6 multiply_reduce_fusion.4
  120.5 0.7 fusion.46
  121.2 0.5 multiply_reduce_fusion
  121.8 0.7 add_multiply_fusion.1
  122.5 0.6 add_convert_fusion.1
  123.2 35.2 %all_gather.1 = bf16[16,1024,128]{2,1,0:T(8,128)(2,1)S(1)} custom-call(bf16[1024,128]{1,0:T(8,128)(2,1)S(1)} %bitcast.62), custom_call_target="tpu_custom_call" | custom-call | tf_op jit(solution)/shard_map/all_gather/pallas_call | solution.py:147
  158.4 2.0 copy-done.3
  160.4 7.4 %copy.32 = bf16[256,64,128]{0,1,2:T(8,128)(2,1)} copy(bf16[256,64,128]{2,1,0:T(8,128)(2,1)} %bitcast.55) | data formatting | bytes 8388608 | tf_op jit(solution)/shard_map/reshape | solution.py:318
  167.8 6.1 %convert_bitcast_fusion.2 = bf16[64,64,128]{1,0,2:T(8,128)(2,1)} fusion(bf16[64,256,128]{1,0,2:T(8,128)(2,1)} %copy.31, bf16[256,64,128]{0,1,2:T(8,128)(2,1)} %copy.32), kind=kOutput, calls=%fused_computation.2 | convolution fusion | flops 268959744 | bytes 9437184 | tf_op jit(solution)/shard_map/jic,kjc->kic/dot_general | solution.py:319
  174.0 3.2 %convert_bitcast_fusion = bf16[64,256,128]{1,0,2:T(8,128)(2,1)} fusion(bf16[64,64,128]{1,0,2:T(8,128)(2,1)S(1)} %copy-done.10, bf16[256,64,128]{0,1,2:T(8,128)(2,1)S(1)} %copy-done.9), kind=kOutput, calls=%fused_computation | convolution fusion | flops 270532608 | bytes 9437184 | tf_op jit(solution)/shard_map/kic,jic->kjc/dot_general | solution.py:320
  177.2 3.3 %copy.33 = bf16[64,64,128]{2,1,0:T(8,128)(2,1)S(1)} copy(bf16[64,64,128]{1,0,2:T(8,128)(2,1)} %convert_bitcast_fusion.2) | data formatting | bytes 2097152 | tf_op jit(solution)/shard_map/convert_element_type | solution.py:323
  180.5 11.1 %left_backward.1 = bf16[4096,128]{1,0:T(8,128)(2,1)} custom-call(s32[1,64]{1,0:T(1,128)S(1)} %bitcast.65, bf16[4096,128]{1,0:T(8,128)(2,1)S(1)} %bitcast.61, bf16[4096,128]{1,0:T(8,128)(2,1)S(1)} %bitcast.59, f32[1,128]{1,0:T(1,128)S(1)} %bitcast.69, f32[1,128]{1,0:T(1,128)S(1)} %bitcast.73, bf16[128,256]{1,0:T(8,128)(2,1)S(1)} %copy.27.both_ref, ...), custom_call_target="tpu_custom_call" | custom-call | tf_op jit(solution)/shard_map/left_backward/pallas_call | solution.py:231
  191.6 6.9 %copy.37 = bf16[64,256,128]{2,1,0:T(8,128)(2,1)} copy(bf16[64,256,128]{1,0,2:T(8,128)(2,1)} %convert_bitcast_fusion) | data formatting | bytes 8388608 | tf_op jit(solution)/shard_map/convert_element_type | solution.py:329
  198.5 2.2 copy-done.4
  200.7 40.8 %right_backward.1 = bf16[16384,128]{1,0:T(8,128)(2,1)} custom-call(s32[1,64]{1,0:T(1,128)S(1)} %bitcast.66, bf16[16384,128]{1,0:T(8,128)(2,1)S(1)} %bitcast.57, bf16[16384,128]{1,0:T(8,128)(2,1)} %bitcast.75, f32[1,128]{1,0:T(1,128)S(1)} %bitcast.70, f32[1,128]{1,0:T(1,128)S(1)} %bitcast.74, bf16[128,256]{1,0:T(8,128)(2,1)S(1)} %copy.24.both_ref, ...), custom_call_target="tpu_custom_call" | custom-call | tf_op jit(solution)/shard_map/right_backward/pallas_call | solution.py:231
  (38 shorter events, 0.5 us)
Async XLA Ops:
  0.6 111.7 %copy-start = (bf16[128,128]{1,0:T(8,128)(2,1)S(1)}, bf16[128,128]{1,0:T(8,128)(2,1)}, u32[]{:S(2)}) copy-start(bf16[128,128]{1,0:T(8,128)(2,1)} %param.31) | copy-start | bytes 98308
  0.6 11.2 %copy-start.7 = (f32[128]{0:T(128)S(1)}, f32[128]{0:T(128)}, u32[]{:S(2)}) copy-start(f32[128]{0:T(128)} %param.23) | copy-start | bytes 1540
  0.7 11.2 %copy-start.8 = (f32[128]{0:T(128)S(1)}, f32[128]{0:T(128)}, u32[]{:S(2)}) copy-start(f32[128]{0:T(128)} %param.24) | copy-start | bytes 1540
  0.7 11.2 %copy-start.6 = (s32[64]{0:T(128)S(1)}, s32[64]{0:T(128)}, u32[]{:S(2)}) copy-start(s32[64]{0:T(128)} %param.35) | copy-start | bytes 772
  0.7 11.2 %copy-start.5 = (bf16[64,64,128]{2,1,0:T(8,128)(2,1)S(1)}, bf16[64,64,128]{2,1,0:T(8,128)(2,1)}, u32[]{:S(2)}) copy-start(bf16[64,64,128]{2,1,0:T(8,128)(2,1)} %param.19) | copy-start | bytes 3145732
  4.9 16.8 %copy-start.14 = (f32[16,64]{1,0:T(8,128)}, f32[16,64]{1,0:T(8,128)S(1)}, u32[]{:S(2)}) copy-start(f32[16,64]{1,0:T(8,128)S(1)} %fusion.43) | copy-start | bytes 12292
  44.8 2.0 copy-start.1
  67.1 2.2 copy-start.2
  69.3 43.1 %copy-start.11 = (bf16[16,64,128]{2,1,0:T(8,128)(2,1)S(1)}, bf16[16,64,128]{2,1,0:T(8,128)(2,1)}, u32[]{:S(2)}) copy-start(bf16[16,64,128]{2,1,0:T(8,128)(2,1)} %param.21) | copy-start | bytes 786436
  111.0 0.6 copy-start.13
  111.7 0.6 copy-start.12
  158.4 2.0 copy-start.3
  167.8 6.1 %copy-start.9 = (bf16[256,64,128]{0,1,2:T(8,128)(2,1)S(1)}, bf16[256,64,128]{0,1,2:T(8,128)(2,1)}, u32[]{:S(2)}) copy-start(bf16[256,64,128]{0,1,2:T(8,128)(2,1)} %copy.32) | copy-start | bytes 12582916
  167.8 6.1 %copy-start.10 = (bf16[64,64,128]{1,0,2:T(8,128)(2,1)S(1)}, bf16[64,64,128]{1,0,2:T(8,128)(2,1)}, u32[]{:S(2)}) copy-start(bf16[64,64,128]{1,0,2:T(8,128)(2,1)} %copy.36) | copy-start | bytes 3145732
  198.5 2.2 copy-start.4

commit v3 on v2

--- a/solution.py
+++ b/solution.py
@@ -10,6 +10,7 @@
 
 MESH = pl.DeviceIdType.MESH
 VMEM_LIMIT = 48 * 1024 * 1024
+UNROLL = 1
 
 
 def bits_of(count):
@@ -166,11 +167,15 @@
     return parts[0] if count == 1 else jnp.concatenate(parts, axis=0)
 
 
+def row_means(values):
+    width = values.shape[-1]
+    share = jnp.full((width, width), 1.0 / width, jnp.bfloat16)
+    return jnp.dot(values.astype(jnp.bfloat16), share, preferred_element_type=jnp.float32)
+
+
 def normed_parts(pair, gain, bias):
-    values = pair.astype(jnp.float32)
-    center = jnp.mean(values, axis=-1, keepdims=True)
-    values = values - center
-    scale = lax.rsqrt(jnp.mean(values * values, axis=-1, keepdims=True) + 1e-05)
+    values = pair.astype(jnp.float32) - row_means(pair)
+    scale = lax.rsqrt(row_means(values * values) + 1e-05)
     unit = values * scale
     return unit, scale, (unit * gain + bias).astype(jnp.bfloat16)
 
@@ -183,11 +188,11 @@
 
 def forward_kernel(rows_ref, pair_ref, gain_ref, bias_ref, both_ref, tile_ref, chain_ref, out_ref):
     inner = chain_ref.shape[0]
-    step = max(inner, min(256, pair_ref.shape[0]))
+    step = max(inner, min(2048, pair_ref.shape[0]))
     ratio = step // inner
     start = pl.program_id(0) * (pair_ref.shape[0] // inner)
 
-    @pl.loop(0, pair_ref.shape[0] // step)
+    @pl.loop(0, pair_ref.shape[0] // step, unroll=UNROLL)
     def _(t):
         at = pl.ds(pl.multiple_of(t * step, step), step)
         unused, unused, normed = normed_parts(pair_ref[at], gain_ref[...], bias_ref[...])
@@ -200,11 +205,11 @@
     rows_ref, pair_ref, grad_ref, gain_ref, bias_ref, both_ref, back_ref, tile_ref, chain_ref, out_ref
 ):
     inner = chain_ref.shape[0]
-    step = max(inner, min(256, pair_ref.shape[0]))
+    step = max(inner, min(2048, pair_ref.shape[0]))
     ratio = step // inner
     start = pl.program_id(0) * (pair_ref.shape[0] // inner)
 
-    @pl.loop(0, pair_ref.shape[0] // step)
+    @pl.loop(0, pair_ref.shape[0] // step, unroll=UNROLL)
     def _(t):
         at = pl.ds(pl.multiple_of(t * step, step), step)
         gain = gain_ref[...]
@@ -219,14 +224,14 @@
         )
         grad_normed = jnp.dot(pulled, back_ref[...], preferred_element_type=jnp.float32)
         grad_unit = grad_normed.astype(jnp.bfloat16).astype(jnp.float32) * gain
-        mean_grad = jnp.mean(grad_unit, axis=-1, keepdims=True)
-        mean_dot = jnp.mean(grad_unit * unit, axis=-1, keepdims=True)
+        mean_grad = row_means(grad_unit)
+        mean_dot = row_means(grad_unit * unit)
         out_ref[at] = (scale * (grad_unit - mean_grad - unit * mean_dot)).astype(jnp.bfloat16)
 
 
 def per_row(kernel, name, streamed, fixed, chain_rows, inner, width):
     rows = streamed[0].shape[0]
-    block = min(rows, 2048)
+    block = min(rows, 4096)
     whole = lambda array: pl.BlockSpec(array.shape, lambda g: (0, 0))
     return pl.pallas_call(
         kernel,

time: 243 us -> 194 us (0.80)
  Pallas kernels: 157 us -> 108 us
    pallas_call x4, Pallas kernels: 81 us -> 31.8 us  [per_row(): pl.pallas_call(kernel, grid=(rows // block,), out_shape=jax.ShapeDtypeStr...]
where the time goes in v3:
time: 194 us; the launch traced here: 192 us
  Pallas kernels  108 us (56%)
  local copies, waits for them, and re-layouts  52.5 us (27%)
  matrix products  21.1 us (11%)
  other arithmetic  9.58 us (5%)
    pallas_call x1, Pallas kernels, reduce_scatter(): pl.pallas_call(functools.partial(scatter_kernel, n), out_shape=jax.ShapeD...  41.1 us
    pallas_call x1, Pallas kernels, all_gather(): pl.pallas_call(functools.partial(gather_kernel, n), out_shape=jax.ShapeDt...  35.2 us
    pallas_call x4, Pallas kernels, per_row(): pl.pallas_call(kernel, grid=(rows // block,), out_shape=jax.ShapeDtypeStr...  31.8 us
    unnamed x34, local copies, waits for them, and re-layouts  13.1 us
    reshape x1, local copies, waits for them, and re-layouts, local(): gathered = gathered.reshape(col_total, slab_rows, hidden)  7.43 us
    convert_element_type x1, local copies, waits for them, and re-layouts, local(): share.astype(jnp.bfloat16)  7.37 us
    convert_element_type x1, local copies, waits for them, and re-layouts, local(): total_right.astype(jnp.bfloat16).reshape(row_total * col_total, hidden)  6.87 us
    reshape x1, local copies, waits for them, and re-layouts, local(): right = per_row(forward_kernel, 'right_forward', [rows_right], [gain, bia...  6.8 us

profile of v3, /device:TPU:11, one launch (start us, length us, event | category | flops | bytes accessed | tf_op | source)
XLA Modules:
  0.0 192.3 jit_solution(580380783596686731)
XLA Ops:
  0.7 0.8 broadcast_in_dim.33
  1.5 0.1 broadcast_in_dim.68
  1.6 0.7 broadcast_in_dim.29
  2.4 1.2 convert_reduce_fusion
  3.6 1.3 fusion.19
  5.0 0.7 broadcast_in_dim.70.chain_ref
  5.7 0.9 copy.25
  6.6 0.9 copy.26
  7.5 0.9 copy.22
  8.4 0.9 copy.23
  9.3 0.1 copy.24.both_ref
  9.4 0.1 copy.27.both_ref
  9.5 0.1 broadcast_in_dim.31.tile_ref
  9.6 0.8 broadcast_in_dim.32.chain_ref
  10.4 1.4 fusion.2
  11.9 2.8 %left_forward.1 = bf16[4096,128]{1,0:T(8,128)(2,1)S(1)} custom-call(s32[1,64]{1,0:T(1,128)S(1)} %bitcast.63, bf16[4096,128]{1,0:T(8,128)(2,1)S(1)} %bitcast.60, f32[1,128]{1,0:T(1,128)S(1)} %bitcast.67, f32[1,128]{1,0:T(1,128)S(1)} %bitcast.71, bf16[128,256]{1,0:T(8,128)(2,1)S(1)} %copy.27.both_ref, s32[64,128]{1,0:T(8,128)S(1)} %broadcast_in_dim.69.tile_ref, ...), custom_call_target="tpu_custom_call" | custom-call | tf_op jit(solution)/shard_map/left_forward/pallas_call | solution.py:236
  14.7 3.8 %copy.36 = bf16[64,64,128]{1,0,2:T(8,128)(2,1)} copy(bf16[64,64,128]{2,1,0:T(8,128)(2,1)S(1)} %bitcast.58) | data formatting | bytes 2097152 | tf_op jit(solution)/shard_map/reshape | solution.py:302
  18.4 10.3 %right_forward.1 = bf16[16384,128]{1,0:T(8,128)(2,1)S(1)} custom-call(s32[1,64]{1,0:T(1,128)S(1)} %bitcast.64, bf16[16384,128]{1,0:T(8,128)(2,1)} %bitcast.56, f32[1,128]{1,0:T(1,128)S(1)} %bitcast.68, f32[1,128]{1,0:T(1,128)S(1)} %bitcast.72, bf16[128,256]{1,0:T(8,128)(2,1)S(1)} %copy.24.both_ref, s32[256,128]{1,0:T(8,128)S(1)} %broadcast_in_dim.31.tile_ref, ...), custom_call_target="tpu_custom_call" | custom-call | tf_op jit(solution)/shard_map/right_forward/pallas_call | solution.py:236
  28.8 2.0 %copy-done.1 = bf16[16384,128]{1,0:T(8,128)(2,1)} copy-done((bf16[16384,128]{1,0:T(8,128)(2,1)}, bf16[16384,128]{1,0:T(8,128)(2,1)S(1)}, u32[]{:S(2)}) %copy-start.1) | copy-done | bytes 4194328
  30.8 6.8 %copy.31 = bf16[64,256,128]{1,0,2:T(8,128)(2,1)} copy(bf16[64,256,128]{2,1,0:T(8,128)(2,1)} %bitcast.53) | data formatting | bytes 8388608 | tf_op jit(solution)/shard_map/reshape | solution.py:306
  37.6 6.1 %convert_bitcast_fusion.1 = bf16[256,64,128]{0,1,2:T(8,128)(2,1)} fusion(bf16[64,64,128]{1,0,2:T(8,128)(2,1)} %copy.36, bf16[64,256,128]{1,0,2:T(8,128)(2,1)} %copy.31), kind=kOutput, calls=%fused_computation.1 | convolution fusion | flops 270532608 | bytes 9437184 | tf_op jit(solution)/shard_map/kic,kjc->jic/dot_general | solution.py:308
  43.7 7.4 %copy.30 = bf16[256,64,128]{2,1,0:T(8,128)(2,1)} copy(bf16[256,64,128]{0,1,2:T(8,128)(2,1)} %convert_bitcast_fusion.1) | data formatting | bytes 8388608 | tf_op jit(solution)/shard_map/convert_element_type | solution.py:310
  51.1 2.2 %copy-done.2 = bf16[256,64,128]{2,1,0:T(8,128)(2,1)S(1)} copy-done((bf16[256,64,128]{2,1,0:T(8,128)(2,1)S(1)}, bf16[256,64,128]{2,1,0:T(8,128)(2,1)}, u32[]{:S(2)}) %copy-start.2) | copy-done | bytes 4194328
  53.3 41.1 %reduce_scatter.1 = f32[1024,128]{1,0:T(8,128)S(1)} custom-call(bf16[16,1024,128]{2,1,0:T(8,128)(2,1)S(1)} %bitcast.54), custom_call_target="tpu_custom_call" | custom-call | tf_op jit(solution)/shard_map/reduce_scatter/pallas_call | solution.py:91
  94.4 0.2 reduce_sum.93
  94.6 0.4 multiply_reduce_fusion.2
  95.0 0.6 copy-done.13
  95.7 0.6 copy-done.12
  96.3 2.5 %multiply_reduce_fusion.3 = (f32[16,64]{1,0:T(8,128)}, f32[16,64]{1,0:T(8,128)}, f32[16,64,128]{2,1,0:T(8,128)S(1)}) fusion(f32[16,64]{1,0:T(8,128)} %copy-done.14, f32[16,64]{1,0:T(8,128)S(1)} %broadcast_multiply_fusion, bf16[16,64,128]{2,1,0:T(8,128)(2,1)S(1)} %copy-done.11, f32[128]{0:T(128)S(1)} %copy-done.7, bf16[128,128]{1,0:T(8,128)(2,1)} %param.32, ...), kind=kOutput, calls=%fused_computation.39 | convolution fusion | flops 69597184 | bytes 2188800 | tf_op jit(solution)/shard_map/transpose(jvp())/dot_general | solution.py:258
  98.9 0.7 multiply_multiply_fusion
  99.6 0.5 fusion.15
  100.1 0.7 add_multiply_fusion
  100.8 2.0 %fusion.18 = bf16[16,64,128]{2,1,0:T(8,128)(2,1)} fusion(bf16[16,64,128]{2,1,0:T(8,128)(2,1)S(1)} %copy-done.11, f32[16,64,128]{2,1,0:T(8,128)S(1)} %get-tuple-element.12, f32[16,64]{1,0:T(8,128)S(1)} %add_multiply_fusion, f32[16,64]{1,0:T(8,128)S(1)} %multiply_multiply_fusion, f32[16,64]{1,0:T(8,128)} %copy-done.14, f32[16,64]{1,0:T(8,128)S(1)} %broadcast_multiply_fusion), kind=kLoop, calls=%fused_computation.28 | loop fusion | flops 917504 | bytes 1064960 | tf_op jit(solution)/shard_map/transpose(jvp())/convert_element_type | solution.py:250
  102.8 1.6 multiply_reduce_fusion.4
  104.5 0.7 fusion.46
  105.2 0.5 multiply_reduce_fusion
  105.8 0.7 add_multiply_fusion.1
  106.5 0.6 add_convert_fusion.1
  107.2 35.2 %all_gather.1 = bf16[16,1024,128]{2,1,0:T(8,128)(2,1)S(1)} custom-call(bf16[1024,128]{1,0:T(8,128)(2,1)S(1)} %bitcast.62), custom_call_target="tpu_custom_call" | custom-call | tf_op jit(solution)/shard_map/all_gather/pallas_call | solution.py:148
  142.4 2.0 %copy-done.3 = bf16[16,1024,128]{2,1,0:T(8,128)(2,1)} copy-done((bf16[16,1024,128]{2,1,0:T(8,128)(2,1)}, bf16[16,1024,128]{2,1,0:T(8,128)(2,1)S(1)}, u32[]{:S(2)}) %copy-start.3) | copy-done | bytes 4194328
  144.4 7.4 %copy.32 = bf16[256,64,128]{0,1,2:T(8,128)(2,1)} copy(bf16[256,64,128]{2,1,0:T(8,128)(2,1)} %bitcast.55) | data formatting | bytes 8388608 | tf_op jit(solution)/shard_map/reshape | solution.py:323
  151.8 6.1 %convert_bitcast_fusion.2 = bf16[64,64,128]{1,0,2:T(8,128)(2,1)} fusion(bf16[64,256,128]{1,0,2:T(8,128)(2,1)} %copy.31, bf16[256,64,128]{0,1,2:T(8,128)(2,1)} %copy.32), kind=kOutput, calls=%fused_computation.2 | convolution fusion | flops 268959744 | bytes 9437184 | tf_op jit(solution)/shard_map/jic,kjc->kic/dot_general | solution.py:324
  158.0 3.2 %convert_bitcast_fusion = bf16[64,256,128]{1,0,2:T(8,128)(2,1)} fusion(bf16[64,64,128]{1,0,2:T(8,128)(2,1)S(1)} %copy-done.10, bf16[256,64,128]{0,1,2:T(8,128)(2,1)S(1)} %copy-done.9), kind=kOutput, calls=%fused_computation | convolution fusion | flops 270532608 | bytes 9437184 | tf_op jit(solution)/shard_map/kic,jic->kjc/dot_general | solution.py:325
  161.2 3.3 %copy.33 = bf16[64,64,128]{2,1,0:T(8,128)(2,1)S(1)} copy(bf16[64,64,128]{1,0,2:T(8,128)(2,1)} %convert_bitcast_fusion.2) | data formatting | bytes 2097152 | tf_op jit(solution)/shard_map/convert_element_type | solution.py:328
  164.5 4.4 %left_backward.1 = bf16[4096,128]{1,0:T(8,128)(2,1)} custom-call(s32[1,64]{1,0:T(1,128)S(1)} %bitcast.65, bf16[4096,128]{1,0:T(8,128)(2,1)S(1)} %bitcast.61, bf16[4096,128]{1,0:T(8,128)(2,1)S(1)} %bitcast.59, f32[1,128]{1,0:T(1,128)S(1)} %bitcast.69, f32[1,128]{1,0:T(1,128)S(1)} %bitcast.73, bf16[128,256]{1,0:T(8,128)(2,1)S(1)} %copy.27.both_ref, ...), custom_call_target="tpu_custom_call" | custom-call | tf_op jit(solution)/shard_map/left_backward/pallas_call | solution.py:236
  169.0 6.9 %copy.37 = bf16[64,256,128]{2,1,0:T(8,128)(2,1)} copy(bf16[64,256,128]{1,0,2:T(8,128)(2,1)} %convert_bitcast_fusion) | data formatting | bytes 8388608 | tf_op jit(solution)/shard_map/convert_element_type | solution.py:334
  175.9 2.2 %copy-done.4 = bf16[64,256,128]{2,1,0:T(8,128)(2,1)S(1)} copy-done((bf16[64,256,128]{2,1,0:T(8,128)(2,1)S(1)}, bf16[64,256,128]{2,1,0:T(8,128)(2,1)}, u32[]{:S(2)}) %copy-start.4) | copy-done | bytes 4194328
  178.0 14.3 %right_backward.1 = bf16[16384,128]{1,0:T(8,128)(2,1)} custom-call(s32[1,64]{1,0:T(1,128)S(1)} %bitcast.66, bf16[16384,128]{1,0:T(8,128)(2,1)S(1)} %bitcast.57, bf16[16384,128]{1,0:T(8,128)(2,1)} %bitcast.75, f32[1,128]{1,0:T(1,128)S(1)} %bitcast.70, f32[1,128]{1,0:T(1,128)S(1)} %bitcast.74, bf16[128,256]{1,0:T(8,128)(2,1)S(1)} %copy.24.both_ref, ...), custom_call_target="tpu_custom_call" | custom-call | tf_op jit(solution)/shard_map/right_backward/pallas_call | solution.py:236
  (38 shorter events, 0.5 us)
Async XLA Ops:
  0.6 95.7 %copy-start = (bf16[128,128]{1,0:T(8,128)(2,1)S(1)}, bf16[128,128]{1,0:T(8,128)(2,1)}, u32[]{:S(2)}) copy-start(bf16[128,128]{1,0:T(8,128)(2,1)} %param.31) | copy-start | bytes 98308
  0.6 11.2 %copy-start.7 = (f32[128]{0:T(128)S(1)}, f32[128]{0:T(128)}, u32[]{:S(2)}) copy-start(f32[128]{0:T(128)} %param.23) | copy-start | bytes 1540
  0.7 11.2 %copy-start.8 = (f32[128]{0:T(128)S(1)}, f32[128]{0:T(128)}, u32[]{:S(2)}) copy-start(f32[128]{0:T(128)} %param.24) | copy-start | bytes 1540
  0.7 11.2 %copy-start.6 = (s32[64]{0:T(128)S(1)}, s32[64]{0:T(128)}, u32[]{:S(2)}) copy-start(s32[64]{0:T(128)} %param.35) | copy-start | bytes 772
  0.7 11.2 %copy-start.5 = (bf16[64,64,128]{2,1,0:T(8,128)(2,1)S(1)}, bf16[64,64,128]{2,1,0:T(8,128)(2,1)}, u32[]{:S(2)}) copy-start(bf16[64,64,128]{2,1,0:T(8,128)(2,1)} %param.19) | copy-start | bytes 3145732
  4.9 13.5 %copy-start.14 = (f32[16,64]{1,0:T(8,128)}, f32[16,64]{1,0:T(8,128)S(1)}, u32[]{:S(2)}) copy-start(f32[16,64]{1,0:T(8,128)S(1)} %fusion.43) | copy-start | bytes 12292
  28.7 2.0 %copy-start.1 = (bf16[16384,128]{1,0:T(8,128)(2,1)}, bf16[16384,128]{1,0:T(8,128)(2,1)S(1)}, u32[]{:S(2)}) copy-start(bf16[16384,128]{1,0:T(8,128)(2,1)S(1)} %right_forward.1) | copy-start | bytes 12582916
  51.1 2.2 %copy-start.2 = (bf16[256,64,128]{2,1,0:T(8,128)(2,1)S(1)}, bf16[256,64,128]{2,1,0:T(8,128)(2,1)}, u32[]{:S(2)}) copy-start(bf16[256,64,128]{2,1,0:T(8,128)(2,1)} %copy.30) | copy-start | bytes 12582916
  53.3 43.1 %copy-start.11 = (bf16[16,64,128]{2,1,0:T(8,128)(2,1)S(1)}, bf16[16,64,128]{2,1,0:T(8,128)(2,1)}, u32[]{:S(2)}) copy-start(bf16[16,64,128]{2,1,0:T(8,128)(2,1)} %param.21) | copy-start | bytes 786436
  95.0 0.6 copy-start.13
  95.7 0.6 copy-start.12
  142.4 2.0 %copy-start.3 = (bf16[16,1024,128]{2,1,0:T(8,128)(2,1)}, bf16[16,1024,128]{2,1,0:T(8,128)(2,1)S(1)}, u32[]{:S(2)}) copy-start(bf16[16,1024,128]{2,1,0:T(8,128)(2,1)S(1)} %all_gather.1) | copy-start | bytes 12582916
  151.8 6.1 %copy-start.9 = (bf16[256,64,128]{0,1,2:T(8,128)(2,1)S(1)}, bf16[256,64,128]{0,1,2:T(8,128)(2,1)}, u32[]{:S(2)}) copy-start(bf16[256,64,128]{0,1,2:T(8,128)(2,1)} %copy.32) | copy-start | bytes 12582916
  151.8 6.1 %copy-start.10 = (bf16[64,64,128]{1,0,2:T(8,128)(2,1)S(1)}, bf16[64,64,128]{1,0,2:T(8,128)(2,1)}, u32[]{:S(2)}) copy-start(bf16[64,64,128]{1,0,2:T(8,128)(2,1)} %copy.36) | copy-start | bytes 3145732
  175.9 2.2 %copy-start.4 = (bf16[64,256,128]{2,1,0:T(8,128)(2,1)S(1)}, bf16[64,256,128]{2,1,0:T(8,128)(2,1)}, u32[]{:S(2)}) copy-start(bf16[64,256,128]{2,1,0:T(8,128)(2,1)} %param.20) | copy-start | bytes 12582916

commit v4 on v3

--- a/solution.py
+++ b/solution.py
@@ -62,7 +62,7 @@
         copies[0, h] = copy(0, h)
         copies[0, h].start()
     rows = x_ref.shape[1]
-    part = min(rows, 128)
+    part = min(rows, 1024)
     for s in range(stages):
         for h in order(s):
             copies[s, h].wait_recv()
@@ -202,7 +202,7 @@
 
 
 def backward_kernel(
-    rows_ref, pair_ref, grad_ref, gain_ref, bias_ref, both_ref, back_ref, tile_ref, chain_ref, out_ref
+    rows_ref, pair_ref, grad_ref, gain_ref, bias_ref, both_ref, tile_ref, chain_ref, out_ref
 ):
     inner = chain_ref.shape[0]
     step = max(inner, min(2048, pair_ref.shape[0]))
@@ -222,7 +222,9 @@
         pulled = jnp.concatenate(
             [grad_value.astype(jnp.bfloat16), grad_gate.astype(jnp.bfloat16)], axis=1
         )
-        grad_normed = jnp.dot(pulled, back_ref[...], preferred_element_type=jnp.float32)
+        grad_normed = lax.dot_general(
+            pulled, both_ref[...], (((1,), (1,)), ((), ())), preferred_element_type=jnp.float32
+        )
         grad_unit = grad_normed.astype(jnp.bfloat16).astype(jnp.float32) * gain
         mean_grad = row_means(grad_unit)
         mean_dot = row_means(grad_unit * unit)
@@ -326,13 +328,13 @@
     grad_left = per_row(
         backward_kernel, "left_backward",
         [rows_left, total_left.astype(jnp.bfloat16).reshape(row_total * slab_rows, hidden)],
-        [gain, bias, both_left, both_left.T, tiles_left, chains_left],
+        [gain, bias, both_left, tiles_left, chains_left],
         chain_rows, slab_rows, channels,
     ).reshape(pair_left.shape)
     grad_right = per_row(
         backward_kernel, "right_backward",
         [rows_right, total_right.astype(jnp.bfloat16).reshape(row_total * col_total, hidden)],
-        [gain, bias, both_right, both_right.T, tiles_right, chains_right],
+        [gain, bias, both_right, tiles_right, chains_right],
         chain_rows, col_total, channels,
     ).reshape(pair_right.shape)
     return (grad_left, grad_right, block_grad)

time: 194 us -> 189 us (0.974)
  other arithmetic: 9.58 us -> 6.09 us
    unnamed x34 -> x38, local copies, waits for them, and re-layouts: 13.1 us -> 12 us
where the time goes in v4:
time: 189 us; the launch traced here: 188 us
  Pallas kernels  108 us (57%)
  local copies, waits for them, and re-layouts  52.7 us (28%)
  matrix products  20.5 us (11%)
  other arithmetic  6.09 us (3%)
    pallas_call x1, Pallas kernels, reduce_scatter(): pl.pallas_call(functools.partial(scatter_kernel, n), out_shape=jax.ShapeD...  41 us
    pallas_call x1, Pallas kernels, all_gather(): pl.pallas_call(functools.partial(gather_kernel, n), out_shape=jax.ShapeDt...  35.2 us
    pallas_call x4, Pallas kernels, per_row(): pl.pallas_call(kernel, grid=(rows // block,), out_shape=jax.ShapeDtypeStr...  31.6 us
    unnamed x38, local copies, waits for them, and re-layouts  12 us
    reshape x1, local copies, waits for them, and re-layouts, local(): gathered = gathered.reshape(col_total, slab_rows, hidden)  7.43 us
    convert_element_type x1, local copies, waits for them, and re-layouts, local(): share.astype(jnp.bfloat16)  7.37 us
    convert_element_type x1, local copies, waits for them, and re-layouts, local(): total_right.astype(jnp.bfloat16).reshape(row_total * col_total, hidden)  6.87 us
    reshape x1, local copies, waits for them, and re-layouts, local(): right = per_row(forward_kernel, 'right_forward', [rows_right], [gain, bia...  6.8 us

profile of v4, /device:TPU:11, one launch (start us, length us, event | category | flops | bytes accessed | tf_op | source)
XLA Modules:
  0.0 188.0 jit_solution(13922921755144341996)
XLA Ops:
  0.7 0.8 broadcast_in_dim.33
  1.5 0.1 broadcast_in_dim.68
  1.6 0.7 broadcast_in_dim.29
  2.3 0.1 broadcast_in_dim.30
  2.4 1.2 convert_reduce_fusion
  3.5 1.3 fusion.19
  4.9 0.1 broadcast_in_dim.69.tile_ref
  5.0 0.7 broadcast_in_dim.70.chain_ref
  5.7 0.8 constant_dynamic-update-slice_fusion.3
  6.5 0.8 constant_dynamic-update-slice_fusion.2.both_ref
  7.2 0.8 constant_dynamic-update-slice_fusion.1
  8.0 0.8 constant_dynamic-update-slice_fusion.both_ref
  8.8 0.1 broadcast_in_dim.31.tile_ref
  8.9 0.8 broadcast_in_dim.32.chain_ref
  9.7 1.4 fusion.2
  11.2 0.6 copy-done.6
  11.8 0.7 copy-done.8
  12.5 0.7 copy-done.10
  13.1 2.8 %left_forward.1 = bf16[4096,128]{1,0:T(8,128)(2,1)S(1)} custom-call(s32[1,64]{1,0:T(1,128)S(1)} %bitcast.59, bf16[4096,128]{1,0:T(8,128)(2,1)S(1)} %bitcast.56, f32[1,128]{1,0:T(1,128)S(1)} %bitcast.63, f32[1,128]{1,0:T(1,128)S(1)} %bitcast.67, bf16[128,256]{1,0:T(8,128)(2,1)S(1)} %constant_dynamic-update-slice_fusion.2.both_ref, ...), custom_call_target="tpu_custom_call" | custom-call | tf_op jit(solution)/shard_map/left_forward/pallas_call | solution.py:238
  15.9 3.8 %copy.29 = bf16[64,64,128]{1,0,2:T(8,128)(2,1)} copy(bf16[64,64,128]{2,1,0:T(8,128)(2,1)S(1)} %bitcast.55) | data formatting | bytes 2097152 | tf_op jit(solution)/shard_map/reshape | solution.py:304
  19.6 10.3 %right_forward.1 = bf16[16384,128]{1,0:T(8,128)(2,1)S(1)} custom-call(s32[1,64]{1,0:T(1,128)S(1)} %bitcast.60, bf16[16384,128]{1,0:T(8,128)(2,1)} %bitcast.52, f32[1,128]{1,0:T(1,128)S(1)} %bitcast.64, f32[1,128]{1,0:T(1,128)S(1)} %bitcast.68, bf16[128,256]{1,0:T(8,128)(2,1)S(1)} %constant_dynamic-update-slice_fusion.both_ref, ...), custom_call_target="tpu_custom_call" | custom-call | tf_op jit(solution)/shard_map/right_forward/pallas_call | solution.py:238
  29.9 2.0 %copy-done.1 = bf16[16384,128]{1,0:T(8,128)(2,1)} copy-done((bf16[16384,128]{1,0:T(8,128)(2,1)}, bf16[16384,128]{1,0:T(8,128)(2,1)S(1)}, u32[]{:S(2)}) %copy-start.1) | copy-done | bytes 4194328
  31.9 6.8 %copy.25 = bf16[64,256,128]{1,0,2:T(8,128)(2,1)} copy(bf16[64,256,128]{2,1,0:T(8,128)(2,1)} %bitcast.49) | data formatting | bytes 8388608 | tf_op jit(solution)/shard_map/reshape | solution.py:308
  38.7 6.1 %convert_bitcast_fusion.1 = bf16[256,64,128]{0,1,2:T(8,128)(2,1)} fusion(bf16[64,64,128]{1,0,2:T(8,128)(2,1)} %copy.29, bf16[64,256,128]{1,0,2:T(8,128)(2,1)} %copy.25), kind=kOutput, calls=%fused_computation.1 | convolution fusion | flops 270532608 | bytes 9437184 | tf_op jit(solution)/shard_map/kic,kjc->jic/dot_general | solution.py:310
  44.9 7.4 %copy.24 = bf16[256,64,128]{2,1,0:T(8,128)(2,1)} copy(bf16[256,64,128]{0,1,2:T(8,128)(2,1)} %convert_bitcast_fusion.1) | data formatting | bytes 8388608 | tf_op jit(solution)/shard_map/convert_element_type | solution.py:312
  52.3 2.2 %copy-done.2 = bf16[256,64,128]{2,1,0:T(8,128)(2,1)S(1)} copy-done((bf16[256,64,128]{2,1,0:T(8,128)(2,1)S(1)}, bf16[256,64,128]{2,1,0:T(8,128)(2,1)}, u32[]{:S(2)}) %copy-start.2) | copy-done | bytes 4194328
  54.5 41.0 %reduce_scatter.1 = f32[1024,128]{1,0:T(8,128)S(1)} custom-call(bf16[16,1024,128]{2,1,0:T(8,128)(2,1)S(1)} %bitcast.50), custom_call_target="tpu_custom_call" | custom-call | tf_op jit(solution)/shard_map/reduce_scatter/pallas_call | solution.py:91
  95.5 0.2 reduce_sum.93
  95.7 0.4 multiply_reduce_fusion.2
  96.1 0.1 add.48
  96.3 1.9 multiply_reduce_fusion.3
  98.2 0.5 fusion.15
  98.7 1.3 fusion.18
  100.0 1.6 multiply_reduce_fusion.4
  101.6 0.1 reduce_sum.114
  101.7 0.5 multiply_reduce_fusion
  102.2 0.1 neg.20
  102.3 0.6 add_convert_fusion.1
  102.9 35.2 %all_gather.1 = bf16[16,1024,128]{2,1,0:T(8,128)(2,1)S(1)} custom-call(bf16[1024,128]{1,0:T(8,128)(2,1)S(1)} %bitcast.58), custom_call_target="tpu_custom_call" | custom-call | tf_op jit(solution)/shard_map/all_gather/pallas_call | solution.py:148
  138.2 2.0 %copy-done.3 = bf16[16,1024,128]{2,1,0:T(8,128)(2,1)} copy-done((bf16[16,1024,128]{2,1,0:T(8,128)(2,1)}, bf16[16,1024,128]{2,1,0:T(8,128)(2,1)S(1)}, u32[]{:S(2)}) %copy-start.3) | copy-done | bytes 4194328
  140.2 7.4 %copy.26 = bf16[256,64,128]{0,1,2:T(8,128)(2,1)} copy(bf16[256,64,128]{2,1,0:T(8,128)(2,1)} %bitcast.51) | data formatting | bytes 8388608 | tf_op jit(solution)/shard_map/reshape | solution.py:325
  147.6 6.1 %convert_bitcast_fusion.2 = bf16[64,64,128]{1,0,2:T(8,128)(2,1)} fusion(bf16[64,256,128]{1,0,2:T(8,128)(2,1)} %copy.25, bf16[256,64,128]{0,1,2:T(8,128)(2,1)} %copy.26), kind=kOutput, calls=%fused_computation.2 | convolution fusion | flops 268959744 | bytes 9437184 | tf_op jit(solution)/shard_map/jic,kjc->kic/dot_general | solution.py:326
  153.8 3.3 %convert_bitcast_fusion = bf16[64,256,128]{1,0,2:T(8,128)(2,1)} fusion(bf16[64,64,128]{1,0,2:T(8,128)(2,1)S(1)} %copy-done.13, bf16[256,64,128]{0,1,2:T(8,128)(2,1)S(1)} %copy-done.12), kind=kOutput, calls=%fused_computation | convolution fusion | flops 270532608 | bytes 9437184 | tf_op jit(solution)/shard_map/kic,jic->kjc/dot_general | solution.py:327
  157.0 3.3 %copy.27 = bf16[64,64,128]{2,1,0:T(8,128)(2,1)S(1)} copy(bf16[64,64,128]{1,0,2:T(8,128)(2,1)} %convert_bitcast_fusion.2) | data formatting | bytes 2097152 | tf_op jit(solution)/shard_map/convert_element_type | solution.py:330
  160.3 4.4 %left_backward.1 = bf16[4096,128]{1,0:T(8,128)(2,1)} custom-call(s32[1,64]{1,0:T(1,128)S(1)} %bitcast.61, bf16[4096,128]{1,0:T(8,128)(2,1)S(1)} %bitcast.57, bf16[4096,128]{1,0:T(8,128)(2,1)S(1)} %bitcast.54, f32[1,128]{1,0:T(1,128)S(1)} %bitcast.65, f32[1,128]{1,0:T(1,128)S(1)} %bitcast.69, ...), custom_call_target="tpu_custom_call" | custom-call | tf_op jit(solution)/shard_map/left_backward/pallas_call | solution.py:238
  164.8 6.9 %copy.30 = bf16[64,256,128]{2,1,0:T(8,128)(2,1)} copy(bf16[64,256,128]{1,0,2:T(8,128)(2,1)} %convert_bitcast_fusion) | data formatting | bytes 8388608 | tf_op jit(solution)/shard_map/convert_element_type | solution.py:336
  171.7 2.2 %copy-done.4 = bf16[64,256,128]{2,1,0:T(8,128)(2,1)S(1)} copy-done((bf16[64,256,128]{2,1,0:T(8,128)(2,1)S(1)}, bf16[64,256,128]{2,1,0:T(8,128)(2,1)}, u32[]{:S(2)}) %copy-start.4) | copy-done | bytes 4194328
  173.8 14.1 %right_backward.1 = bf16[16384,128]{1,0:T(8,128)(2,1)} custom-call(s32[1,64]{1,0:T(1,128)S(1)} %bitcast.62, bf16[16384,128]{1,0:T(8,128)(2,1)S(1)} %bitcast.53, bf16[16384,128]{1,0:T(8,128)(2,1)} %bitcast.71, f32[1,128]{1,0:T(1,128)S(1)} %bitcast.66, f32[1,128]{1,0:T(1,128)S(1)} %bitcast.70, bf16[128,256]{1,0:T(8,128)(2,1)S(1)} %constant_dynamic-update-slice_fusion.both_ref, ...), custom_call_target="tpu_custom_call" | custom-call | tf_op jit(solution)/shard_map/right_backward/pallas_call | solution.py:238
  (40 shorter events, 0.2 us)
Async XLA Ops:
  0.6 95.6 %copy-start = (bf16[128,128]{1,0:T(8,128)(2,1)S(1)}, bf16[128,128]{1,0:T(8,128)(2,1)}, u32[]{:S(2)}) copy-start(bf16[128,128]{1,0:T(8,128)(2,1)} %param.31) | copy-start | bytes 98308
  0.6 10.5 %copy-start.5 = (bf16[64,64,128]{2,1,0:T(8,128)(2,1)S(1)}, bf16[64,64,128]{2,1,0:T(8,128)(2,1)}, u32[]{:S(2)}) copy-start(bf16[64,64,128]{2,1,0:T(8,128)(2,1)} %param.19) | copy-start | bytes 3145732
  8.9 10.8 %copy-start.7 = (s32[64]{0:T(128)S(1)}, s32[64]{0:T(128)}, u32[]{:S(2)}) copy-start(s32[64]{0:T(128)} %param.35) | copy-start | bytes 772
  8.9 10.8 %copy-start.9 = (f32[128]{0:T(128)S(1)}, f32[128]{0:T(128)}, u32[]{:S(2)}) copy-start(f32[128]{0:T(128)} %param.23) | copy-start | bytes 1540
  8.9 10.8 %copy-start.11 = (f32[128]{0:T(128)S(1)}, f32[128]{0:T(128)}, u32[]{:S(2)}) copy-start(f32[128]{0:T(128)} %param.24) | copy-start | bytes 1540
  11.2 0.7 copy-start.6
  11.8 0.7 copy-start.8
  12.5 0.7 copy-start.10
  29.9 2.0 %copy-start.1 = (bf16[16384,128]{1,0:T(8,128)(2,1)}, bf16[16384,128]{1,0:T(8,128)(2,1)S(1)}, u32[]{:S(2)}) copy-start(bf16[16384,128]{1,0:T(8,128)(2,1)S(1)} %right_forward.1) | copy-start | bytes 12582916
  52.2 44.0 %copy-start.15 = (f32[128]{0:T(128)S(1)}, f32[128]{0:T(128)}, u32[]{:S(2)}) copy-start(f32[128]{0:T(128)} %param.29) | copy-start | bytes 1540
  52.2 44.0 %copy-start.17 = (f32[128]{0:T(128)S(1)}, f32[128]{0:T(128)}, u32[]{:S(2)}) copy-start(f32[128]{0:T(128)} %param.30) | copy-start | bytes 1540
  52.2 2.2 %copy-start.2 = (bf16[256,64,128]{2,1,0:T(8,128)(2,1)S(1)}, bf16[256,64,128]{2,1,0:T(8,128)(2,1)}, u32[]{:S(2)}) copy-start(bf16[256,64,128]{2,1,0:T(8,128)(2,1)} %copy.24) | copy-start | bytes 12582916
  54.5 41.8 %copy-start.14 = (bf16[16,64,128]{2,1,0:T(8,128)(2,1)S(1)}, bf16[16,64,128]{2,1,0:T(8,128)(2,1)}, u32[]{:S(2)}) copy-start(bf16[16,64,128]{2,1,0:T(8,128)(2,1)} %param.21) | copy-start | bytes 786436
  54.5 41.8 %copy-start.16 = (bf16[128,128]{1,0:T(8,128)(2,1)S(1)}, bf16[128,128]{1,0:T(8,128)(2,1)}, u32[]{:S(2)}) copy-start(bf16[128,128]{1,0:T(8,128)(2,1)} %param.32) | copy-start | bytes 98308
  138.2 2.0 %copy-start.3 = (bf16[16,1024,128]{2,1,0:T(8,128)(2,1)}, bf16[16,1024,128]{2,1,0:T(8,128)(2,1)S(1)}, u32[]{:S(2)}) copy-start(bf16[16,1024,128]{2,1,0:T(8,128)(2,1)S(1)} %all_gather.1) | copy-start | bytes 12582916
  147.6 6.1 %copy-start.12 = (bf16[256,64,128]{0,1,2:T(8,128)(2,1)S(1)}, bf16[256,64,128]{0,1,2:T(8,128)(2,1)}, u32[]{:S(2)}) copy-start(bf16[256,64,128]{0,1,2:T(8,128)(2,1)} %copy.26) | copy-start | bytes 12582916
  147.6 6.1 %copy-start.13 = (bf16[64,64,128]{1,0,2:T(8,128)(2,1)S(1)}, bf16[64,64,128]{1,0,2:T(8,128)(2,1)}, u32[]{:S(2)}) copy-start(bf16[64,64,128]{1,0,2:T(8,128)(2,1)} %copy.29) | copy-start | bytes 3145732
  171.7 2.2 %copy-start.4 = (bf16[64,256,128]{2,1,0:T(8,128)(2,1)S(1)}, bf16[64,256,128]{2,1,0:T(8,128)(2,1)}, u32[]{:S(2)}) copy-start(bf16[64,256,128]{2,1,0:T(8,128)(2,1)} %param.20) | copy-start | bytes 12582916
